TPU v7x, 256 devices: a whole 4x4x8 slice. The times are simulated.
256 devices in a mesh: seq: 64 (over x, z, y_lo), head: 4 (over y_hi, core).
Axes of the slice: x: 4, y: 4 (y_hi: 2, y_lo: 2; y = y_hi * 2 + y_lo), z: 8, core: 2. Of those that a mesh axis runs over, the one named last changes fastest.
Arguments:
- inputs: bfloat16 [131072, 1024], P('seq'), may hold values from -32 to 32
- latent_array: bfloat16 [2048, 1024], P('seq'), may hold values from -16 to 16
- w_query: bfloat16 [1024, 1024], P(None, 'head'), may hold values from -4 to 4
- w_key: bfloat16 [1024, 1024], P(None, 'head'), may hold values from -4 to 4
- w_value: bfloat16 [1024, 1024], P(None, 'head'), may hold values from -0.1875 to 0.1875
- w_out: bfloat16 [1024, 1024], P('head'), may hold values from -0.1875 to 0.1875
- w_up: bfloat16 [1024, 4096], P(None, 'head'), may hold values from -0.1875 to 0.1875
- w_down: bfloat16 [4096, 1024], P('head'), may hold values from -0.09375 to 0.09375
Outputs:
- latent_out: bfloat16 [2048, 1024], P('seq', 'head')
All inputs are finite; a program needn't handle non-finite values.
Results may differ from a plain program's by a relative error of at most 0.01355.
The roundings to bfloat16 on the way count: a program that leaves them out, or rounds other values in their place, can miss the bound.
Values may be sent and summed in bfloat16 or wider, within the bound.
No kernel may reach another device: no remote copies, remote signals or barrier semaphores. Data moves between devices by JAX's collectives and lax.ppermute only.
A program may use at most 320 MiB of HBM per device.

v0:
```python
import functools

import jax
import jax.numpy as jnp
from jax import lax
from jax.experimental import pallas as pl
from jax.experimental.pallas import tpu as pltpu
from jax.sharding import Mesh
from jax.sharding import PartitionSpec as P

HEAD_DIM = 64
HEADS_HERE = 4
LEVEL_ROWS = 16
LANES = 128
SEQ = ("x", "z", "ylo")
HEAD = ("yhi", "core")
BF16 = jnp.bfloat16
F32 = jnp.float32
NT = (((1,), (1,)), ((), ()))
NN = (((1,), (0,)), ((), ()))
TN = (((0,), (0,)), ((), ()))


def product(left, right, numbers=NN):
    return lax.dot_general(left, right, numbers, preferred_element_type=F32)


def params(mib):
    return pltpu.CompilerParams(vmem_limit_bytes=mib * 2**20)


def norm_rows(widened):
    width = widened.shape[-1]
    row_mean = jnp.sum(widened, axis=-1, keepdims=True) / width
    row_square = jnp.sum(widened * widened, axis=-1, keepdims=True) / width
    row_var = row_square - row_mean * row_mean
    return (widened - row_mean) * lax.rsqrt(row_var + 1e-05)


def in_hbm(value):
    return pltpu.with_memory_space_constraint(value, pltpu.HBM)


def query_kernel(latent_hbm, w_hbm, out_ref, latent_ref, w_ref, sems):
    copies = [
        pltpu.make_async_copy(latent_hbm, latent_ref, sems.at[0]),
        pltpu.make_async_copy(w_hbm, w_ref, sems.at[1]),
    ]
    for copy in copies:
        copy.start()
    copies[0].wait()
    normed = norm_rows(latent_ref[...].astype(F32)).astype(BF16)
    copies[1].wait()
    out_ref[...] = (product(normed, w_ref[...]) * HEAD_DIM ** (-0.5)).astype(BF16)


def make_queries(latent, w_query):
    return pl.pallas_call(
        query_kernel,
        in_specs=[pl.BlockSpec(memory_space=pltpu.HBM)] * 2,
        out_shape=jax.ShapeDtypeStruct((latent.shape[0], w_query.shape[1]), BF16),
        scratch_shapes=[
            pltpu.VMEM(latent.shape, BF16),
            pltpu.VMEM(w_query.shape, BF16),
            pltpu.SemaphoreType.DMA((2,)),
        ],
        compiler_params=params(8),
        name="make_queries",
    )(in_hbm(latent), in_hbm(w_query))


def key_value_kernel(
    block, x_hbm, w_key_hbm, w_value_hbm, key_ref, value_ref, x_ref, w_key_ref, w_value_ref, sems
):
    tokens = x_ref.shape[0]
    weights = [
        pltpu.make_async_copy(w_key_hbm, w_key_ref, sems.at[0]),
        pltpu.make_async_copy(w_value_hbm, w_value_ref, sems.at[1]),
    ]
    spans = [slice(start, start + block) for start in range(0, tokens, block)]
    copies = [
        pltpu.make_async_copy(x_hbm.at[span], x_ref.at[span], sems.at[2 + i])
        for i, span in enumerate(spans)
    ]
    for copy in copies[:1] + weights + copies[1:]:
        copy.start()
    lane = lax.broadcasted_iota(jnp.int32, (block, LANES), 1)
    low = lane < HEAD_DIM
    for i, span in enumerate(spans):
        copies[i].wait()
        normed = norm_rows(x_ref[span].astype(F32)).astype(BF16)
        if i == 0:
            weights[0].wait()
            weights[1].wait()
        keys = product(normed, w_key_ref[...]).astype(BF16)
        vals = product(normed, w_value_ref[...])
        for head in range(HEADS_HERE):
            key_ref[head, span] = keys[:, head * HEAD_DIM : (head + 1) * HEAD_DIM]
            pair = vals[:, head // 2 * LANES : (head // 2 + 1) * LANES]
            one = jnp.where(lane == (HEAD_DIM if head % 2 == 0 else 0), 1.0, 0.0)
            kept = jnp.where(low, pair, one) if head % 2 == 0 else jnp.where(low, one, pair)
            value_ref[head, span] = kept.astype(BF16)


def make_keys_values(x, w_key, w_value):
    tokens = x.shape[0]
    block = 512
    return pl.pallas_call(
        functools.partial(key_value_kernel, block),
        in_specs=[pl.BlockSpec(memory_space=pltpu.HBM)] * 3,
        out_shape=[
            jax.ShapeDtypeStruct((HEADS_HERE, tokens, HEAD_DIM), BF16),
            jax.ShapeDtypeStruct((HEADS_HERE, tokens, LANES), BF16),
        ],
        scratch_shapes=[
            pltpu.VMEM(x.shape, BF16),
            pltpu.VMEM(w_key.shape, BF16),
            pltpu.VMEM(w_value.shape, BF16),
            pltpu.SemaphoreType.DMA((2 + tokens // block,)),
        ],
        compiler_params=params(16),
        name="make_keys_values",
    )(in_hbm(x), in_hbm(w_key), in_hbm(w_value))


def split_levels(levels, lane):
    first = levels.astype(BF16).astype(F32)
    rest = levels - first
    second = rest.astype(BF16).astype(F32)
    third = rest - second
    parts = jnp.where(lane < 4, first, jnp.where(lane < 8, second, third))
    return jnp.where(lane < 12, parts, 0.0)


def level_rows(rows):
    return rows // (2 * LANES) * LEVEL_ROWS


def attend_kernel(count, *refs):
    query_refs, (key_ref, value_ref) = refs[:count], refs[count : count + 2]
    out_refs = refs[count + 2 :]
    rows = query_refs[0].shape[0]
    total_rows = rows * count

    def scores_of(head):
        columns = slice(head * HEAD_DIM, (head + 1) * HEAD_DIM)
        parts = [ref[:, columns] for ref in query_refs]
        part = parts[0] if count == 1 else jnp.concatenate(parts, axis=0)
        return product(part, key_ref[head], NT)

    lane = lax.broadcasted_iota(jnp.int32, (total_rows, LANES), 1)
    levels = jnp.zeros((total_rows, LANES), F32)
    following = scores_of(0)
    even = None
    for head in range(HEADS_HERE):
        scores = following
        if head + 1 < HEADS_HERE:
            following = scores_of(head + 1)
        highest = jnp.max(scores, axis=1, keepdims=True)
        weights = jnp.exp(scores - highest).astype(BF16)
        accum = product(weights, value_ref[head])
        place = HEAD_DIM if head % 2 == 0 else 0
        total = accum[:, place : place + 1]
        mean = accum * (1.0 / total)
        levels = jnp.where(lane % 4 == head, highest + jnp.log(total), levels)
        if head % 2 == 0:
            even = mean
        else:
            both = jnp.where(lane < HEAD_DIM, even, mean).astype(BF16)
            for i, ref in enumerate(out_refs):
                columns = slice(head // 2 * LANES, (head // 2 + 1) * LANES)
                ref[:rows, columns] = both[i * rows : (i + 1) * rows]
    packed = jnp.transpose(split_levels(levels, lane))[:LEVEL_ROWS].astype(BF16)
    for i, ref in enumerate(out_refs):
        for j in range(rows // (2 * LANES)):
            start = i * rows + j * 2 * LANES
            span = slice(rows + j * LEVEL_ROWS, rows + (j + 1) * LEVEL_ROWS)
            ref[span] = packed[:, start : start + 2 * LANES]


def attend(chunks, keys, values):
    count = len(chunks)
    rows = chunks[0].shape[0]
    return pl.pallas_call(
        functools.partial(attend_kernel, count),
        out_shape=[jax.ShapeDtypeStruct((rows + level_rows(rows), 2 * LANES), BF16)] * count,
        compiler_params=params(20),
        name="attend",
    )(*chunks, keys, values)


def spread_matrix(count):
    source = lax.broadcasted_iota(jnp.int32, (count, 2 * LANES), 0)
    target = lax.broadcasted_iota(jnp.int32, (count, 2 * LANES), 1)
    hit = (source < 12) & (source % 4 == target // HEAD_DIM)
    return jnp.where(hit, 1.0, 0.0).astype(BF16)


def side_levels(piece):
    return piece[:, : 2 * LANES], product(piece[:, 2 * LANES :], spread_matrix(LANES))


def under_levels(piece):
    rows = piece.shape[0] * 2 * LANES // (2 * LANES + LEVEL_ROWS)
    spread = spread_matrix(LEVEL_ROWS)
    levels = [
        product(piece[start : start + LEVEL_ROWS], spread, TN)
        for start in range(rows, piece.shape[0], LEVEL_ROWS)
    ]
    return piece[:rows], jnp.concatenate(levels, axis=0)


def merged(pieces, read):
    means, levels = zip(*[read(piece) for piece in pieces])
    highest = functools.reduce(jnp.maximum, levels)
    total, accum = None, None
    for mean, level in zip(means, levels):
        factor = jnp.exp(level - highest)
        term = factor * mean.astype(F32)
        total = factor if total is None else total + factor
        accum = term if accum is None else accum + term
    return accum / total, highest, total


def merge_kernel(count, read, *refs):
    out_refs = refs[count:]
    pieces = [ref[...] for ref in refs[:count]]
    if count == 1:
        pieces = [pieces[0][i] for i in range(pieces[0].shape[0])]
    mean, highest, total = merged(pieces, read)
    levels = highest + jnp.log(total)
    lane = lax.broadcasted_iota(jnp.int32, (levels.shape[0], LANES), 1)
    one, two = levels[:, :LANES], levels[:, LANES:]
    one_other, two_other = pltpu.roll(one, HEAD_DIM, 1), pltpu.roll(two, HEAD_DIM, 1)
    head = lane % 4
    picked = jnp.where(
        head == 0, one, jnp.where(head == 1, one_other, jnp.where(head == 2, two, two_other))
    )
    packed = split_levels(picked, lane).astype(BF16)
    rows = out_refs[0].shape[0]
    for i, ref in enumerate(out_refs):
        span = slice(i * rows, (i + 1) * rows)
        ref[:, : 2 * LANES] = mean[span].astype(BF16)
        ref[:, 2 * LANES :] = packed[span]


def merge(pieces, read, rows, parts):
    return pl.pallas_call(
        functools.partial(merge_kernel, len(pieces), read),
        out_shape=[jax.ShapeDtypeStruct((rows // parts, 3 * LANES), BF16)] * parts,
        compiler_params=params(24),
        name="merge",
    )(*pieces)


def project_kernel(count, *refs):
    w_ref, out_ref = refs[count:]
    mean, highest, total = merged([ref[...] for ref in refs[:count]], side_levels)
    projected = product(mean.astype(BF16), w_ref[...])
    columns = out_ref.shape[2]
    for i in range(out_ref.shape[0]):
        out_ref[i] = projected[:, i * columns : (i + 1) * columns]


def project(pieces, w_out):
    rows, width = pieces[0].shape[0], w_out.shape[1]
    return pl.pallas_call(
        functools.partial(project_kernel, len(pieces)),
        out_shape=jax.ShapeDtypeStruct((2, rows, width // 2), F32),
        compiler_params=params(8),
        name="project",
    )(*pieces, w_out)


def placed_call(kernel, name, out_shape, place, *operands):
    return pl.pallas_call(
        kernel,
        in_specs=[pl.BlockSpec(memory_space=pltpu.SMEM)]
        + [pl.BlockSpec(memory_space=pltpu.VMEM)] * len(operands),
        out_shape=out_shape,
        compiler_params=params(8),
        name=name,
    )(place, *operands)


def add_kernel(core_ref, halves_ref, other_ref, out_ref):
    out_ref[...] = halves_ref[core_ref[0]] + other_ref[...]


def residual_kernel(core_ref, one_ref, two_ref, latent_ref, out_ref):
    columns = out_ref.shape[1]
    own = latent_ref[:, pl.ds(pl.multiple_of(core_ref[0] * columns, LANES), columns)]
    out_ref[...] = (own.astype(F32) + (one_ref[...] + two_ref[...])).astype(BF16)


def mlp_kernel(core_ref, own_ref, other_ref, w_up_hbm, w_down_hbm, *refs):
    resid_ref, share_ref, w_up_ref, w_down_ref, sems = refs
    copies = [
        pltpu.make_async_copy(w_up_hbm, w_up_ref, sems.at[0]),
        pltpu.make_async_copy(w_down_hbm, w_down_ref, sems.at[1]),
    ]
    for copy in copies:
        copy.start()
    columns = resid_ref.shape[2]
    own, other = own_ref[...], other_ref[...]
    low = core_ref[0] == 0
    residual = jnp.concatenate([jnp.where(low, own, other), jnp.where(low, other, own)], axis=1)
    normed = norm_rows(residual.astype(F32)).astype(BF16)
    copies[0].wait()
    raised = product(normed, w_up_ref[...])
    hidden = (0.5 * raised * (1.0 + lax.erf(raised * 0.5**0.5))).astype(BF16)
    copies[1].wait()
    share = product(hidden, w_down_ref[...]).astype(BF16)
    for high in range(2):
        for core in range(2):
            i = high * 2 + core
            resid_ref[i] = residual[:, i * columns : (i + 1) * columns]
            share_ref[core, high] = share[:, i * columns : (i + 1) * columns]


def mlp(core, own, other, w_up, w_down):
    rows, half = own.shape
    vmem, hbm = pl.BlockSpec(memory_space=pltpu.VMEM), pl.BlockSpec(memory_space=pltpu.HBM)
    return pl.pallas_call(
        mlp_kernel,
        in_specs=[pl.BlockSpec(memory_space=pltpu.SMEM), vmem, vmem, hbm, hbm],
        out_shape=[
            jax.ShapeDtypeStruct((4, rows, half // 2), BF16),
            jax.ShapeDtypeStruct((2, 2, rows, half // 2), BF16),
        ],
        scratch_shapes=[
            pltpu.VMEM(w_up.shape, BF16),
            pltpu.VMEM(w_down.shape, BF16),
            pltpu.SemaphoreType.DMA((2,)),
        ],
        compiler_params=params(16),
        name="mlp",
    )(core, own, other, in_hbm(w_up), in_hbm(w_down))


def pair_kernel(place_ref, shares_ref, other_ref, kept_ref, sent_ref):
    high, core = place_ref[0], place_ref[1]
    for ref, index in ((kept_ref, high), (sent_ref, 1 - high)):
        ref[...] = shares_ref[core, index].astype(F32) + other_ref[index].astype(F32)


def close_kernel(place_ref, resid_ref, kept_ref, other_ref, out_ref):
    own = resid_ref[place_ref[0] * 2 + place_ref[1]]
    out_ref[...] = (own.astype(F32) + (kept_ref[...] + other_ref[...])).astype(BF16)


def along(value, axis, by):
    size = lax.axis_size(axis)
    return lax.ppermute(value, axis, [(i, (i + by) % size) for i in range(size)])


def swapped(value, axes, bits):
    size = lax.axis_size(axes)
    return lax.ppermute(value, axes, [(i, i ^ bits) for i in range(size)])


STEPS = (2, 1, 3)


def on_device(inputs, latent, w_query, w_key, w_value, w_out, w_up, w_down):
    queries = make_queries(latent, w_query)
    rows, columns = queries.shape
    count = lax.axis_size("z")
    both = jnp.concatenate([queries, swapped(queries, "ylo", 1)], axis=0)
    spread = jnp.broadcast_to(both[None], (count,) + both.shape)
    part = lax.all_to_all(spread, "z", 0, 0, tiled=True).reshape(count * 2 * rows, columns)
    arrived = [along(part, "x", by) for by in STEPS]
    inputs, part = lax.optimization_barrier((inputs, part))
    keys, values = make_keys_values(inputs, w_key, w_value)
    pieces = []
    for by, chunk in zip(STEPS, arrived):
        pieces.append(along(attend([chunk], keys, values)[0], "x", -by))
    pieces.append(attend([part], keys, values)[0])
    block = merge(pieces, under_levels, part.shape[0], 1)[0]
    block = lax.all_to_all(block.reshape(count, 2 * rows, -1), "z", 0, 0, tiled=True)
    own, others = merge([block], side_levels, 2 * rows, 2)
    pieces = [own, swapped(others, "ylo", 1)]
    high, core = lax.axis_index("yhi"), lax.axis_index("core")
    place = jnp.stack([high, core]).astype(jnp.int32)
    core_place = place[1:]
    width = latent.shape[1]
    half = jax.ShapeDtypeStruct((rows, width // 2), F32)
    quarter = jax.ShapeDtypeStruct((rows, width // 4), F32)
    halves = project(pieces, w_out)
    other = swapped(lax.dynamic_index_in_dim(halves, 1 - core, 0, keepdims=False), HEAD, 1)
    pair = placed_call(add_kernel, "pair_sum", half, core_place, halves, other)
    across = swapped(pair, HEAD, 2)
    resid_half = placed_call(
        residual_kernel,
        "residual",
        jax.ShapeDtypeStruct(half.shape, BF16),
        core_place,
        pair,
        across,
        latent,
    )
    resid, shares = mlp(core_place, resid_half, swapped(resid_half, HEAD, 1), w_up, w_down)
    other = swapped(lax.dynamic_index_in_dim(shares, 1 - core, 0, keepdims=False), HEAD, 1)
    kept, sent = placed_call(pair_kernel, "pair_shares", [quarter] * 2, place, shares, other)
    return placed_call(
        close_kernel,
        "close",
        jax.ShapeDtypeStruct(quarter.shape, BF16),
        place,
        resid,
        kept,
        swapped(sent, HEAD, 2),
    )


def solution(mesh):
    fine = Mesh(mesh.devices.reshape(4, 8, 2, 2, 2), SEQ + HEAD)
    placed = (
        P(SEQ, None),
        P(SEQ, None),
        P(None, HEAD),
        P(None, HEAD),
        P(None, HEAD),
        P(HEAD, None),
        P(None, HEAD),
        P(HEAD, None),
    )
    return jax.shard_map(
        on_device, mesh=fine, in_specs=placed, out_specs=P(SEQ, HEAD), check_vma=False
    )
```

profile of v0, /device:TPU:1, one launch (start us, length us, event | category | flops | bytes accessed | tf_op | source)
XLA Modules:
  0.0 102.4 jit_solution(3155647492240775038)
XLA Ops:
  0.0 1.3 %make_queries.1 = bf16[32,256]{1,0:T(8,128)(2,1)S(1)} custom-call(bf16[32,1024]{1,0:T(8,128)(2,1)} %latent_ref.1, bf16[1024,256]{1,0:T(8,128)(2,1)} %w_hbm.1), custom_call_target="tpu_custom_call" | custom-call | tf_op jit(solution)/shard_map/make_queries/pallas_call | solution.py:58
  1.3 2.2 %collective-permute-start = (bf16[32,256]{1,0:T(8,128)(2,1)S(1)}, bf16[32,256]{1,0:T(8,128)(2,1)S(1)}, u32[]{:S(2)}, u32[]{:S(2)}) collective-permute-start(bf16[32,256]{1,0:T(8,128)(2,1)S(1)} %make_queries.1), channel_id=1, source_target_pairs={{0,4},{4,0},{1,5},{5,1},{2,6},{6,2},{3,7},{7,3},{8,12},{12,8},{9,1... | collective-permute-start | bytes 49160 | tf_op jit(solution)/shard_map/ppermute | solution.py:359
  3.5 1.1 %collective-permute-done = bf16[32,256]{1,0:T(8,128)(2,1)S(1)} collective-permute-done((bf16[32,256]{1,0:T(8,128)(2,1)S(1)}, bf16[32,256]{1,0:T(8,128)(2,1)S(1)}, u32[]{:S(2)}, u32[]{:S(2)}) %collective-permute-start) | collective-permute-done | bytes 16416 | tf_op jit(solution)/shard_map/ppermute | solution.py:359
  4.7 17.4 %all_to_all.10 = bf16[8,64,256]{2,1,0:T(8,128)(2,1)S(1)} all-to-all(bf16[8,64,256]{2,1,0:T(8,128)(2,1)S(1)} %broadcast_in_dim.2), channel_id=1, replica_groups=mesh['x'=4,'z'=8,'ylo'=2,'yhi'=2,'core'=2] {'z'}, dimensions={0} | all-to-all | bytes 524288 | tf_op jit(solution)/shard_map/all_to_all | solution.py:371
  22.1 2.7 %collective-permute-start.1 = (bf16[512,256]{1,0:T(8,128)(2,1)S(1)}, bf16[512,256]{1,0:T(8,128)(2,1)S(1)}, u32[]{:S(2)}, u32[]{:S(2)}) collective-permute-start(bf16[512,256]{1,0:T(8,128)(2,1)S(1)} %bitcast.9), channel_id=1, source_target_pairs={{0,128},{64,192},{128,0},{192,64},{1,129},{65,193},{129,1},{193,65... | collective-permute-start | bytes 786440 | tf_op jit(solution)/shard_map/ppermute | solution.py:354
  25.1 2.4 %collective-permute-start.5 = (bf16[512,256]{1,0:T(8,128)(2,1)S(1)}, bf16[512,256]{1,0:T(8,128)(2,1)S(1)}, u32[]{:S(2)}, u32[]{:S(2)}) collective-permute-start(bf16[512,256]{1,0:T(8,128)(2,1)S(1)} %bitcast.11), channel_id=1, source_target_pairs={{0,192},{64,0},{128,64},{192,128},{1,193},{65,1},{129,65},{193,129... | collective-permute-start | bytes 786440 | tf_op jit(solution)/shard_map/ppermute | solution.py:354
  27.5 5.7 %make_keys_values.1 = (bf16[4,2048,64]{2,1,0:T(8,128)(2,1)S(1)}, bf16[4,2048,128]{2,1,0:T(8,128)(2,1)S(1)}) custom-call(bf16[2048,1024]{1,0:T(8,128)(2,1)} %x_hbm, bf16[1024,256]{1,0:T(8,128)(2,1)} %w_key_hbm.1, bf16[1024,256]{1,0:T(8,128)(2,1)} %w_value_hbm.1), custom_call_target="tpu_custom_call" | custom-call | tf_op jit(solution)/shard_map/make_keys_values/pallas_call | solution.py:108
  33.2 5.3 %attend.4 = bf16[544,256]{1,0:T(8,128)(2,1)S(1)} custom-call(bf16[512,256]{1,0:T(8,128)(2,1)S(1)} %collective-permute-done.1.refs_0_, bf16[4,2048,64]{2,1,0:T(8,128)(2,1)S(1)} %get-tuple-element.16.refs_1_, bf16[4,2048,128]{2,1,0:T(8,128)(2,1)S(1)} %get-tuple-element.17.refs_2_), custom_call_target="tpu_custom_call" | custom-call | tf_op jit(solution)/shard_map/attend/pallas_call | solution.py:184
  38.8 5.3 %attend.5 = bf16[544,256]{1,0:T(8,128)(2,1)S(1)} custom-call(bf16[512,256]{1,0:T(8,128)(2,1)S(1)} %collective-permute-done.3.refs_0_, bf16[4,2048,64]{2,1,0:T(8,128)(2,1)S(1)} %get-tuple-element.16.refs_1_, bf16[4,2048,128]{2,1,0:T(8,128)(2,1)S(1)} %get-tuple-element.17.refs_2_), custom_call_target="tpu_custom_call" | custom-call | tf_op jit(solution)/shard_map/attend/pallas_call | solution.py:184
  44.1 1.5 %collective-permute-start.4 = (bf16[544,256]{1,0:T(8,128)(2,1)S(1)}, bf16[544,256]{1,0:T(8,128)(2,1)S(1)}, u32[]{:S(2)}, u32[]{:S(2)}) collective-permute-start(bf16[544,256]{1,0:T(8,128)(2,1)S(1)} %attend.5), channel_id=1, source_target_pairs={{0,192},{64,0},{128,64},{192,128},{1,193},{65,1},{129,65},{193,129... | collective-permute-start | bytes 835592 | tf_op jit(solution)/shard_map/ppermute | solution.py:354
  45.7 5.3 %attend.6 = bf16[544,256]{1,0:T(8,128)(2,1)S(1)} custom-call(bf16[512,256]{1,0:T(8,128)(2,1)S(1)} %collective-permute-done.5.refs_0_, bf16[4,2048,64]{2,1,0:T(8,128)(2,1)S(1)} %get-tuple-element.16.refs_1_, bf16[4,2048,128]{2,1,0:T(8,128)(2,1)S(1)} %get-tuple-element.17.refs_2_), custom_call_target="tpu_custom_call" | custom-call | tf_op jit(solution)/shard_map/attend/pallas_call | solution.py:184
  51.0 0.3 collective-permute-start.6
  51.3 5.3 %attend.7.refs_3_ = bf16[544,256]{1,0:T(8,128)(2,1)S(1)} custom-call(bf16[512,256]{1,0:T(8,128)(2,1)S(1)} %bitcast.12, bf16[4,2048,64]{2,1,0:T(8,128)(2,1)S(1)} %get-tuple-element.16.refs_1_, bf16[4,2048,128]{2,1,0:T(8,128)(2,1)S(1)} %get-tuple-element.17.refs_2_), custom_call_target="tpu_custom_call" | custom-call | tf_op jit(solution)/shard_map/attend/pallas_call | solution.py:184
  56.7 1.2 %collective-permute-done.6.refs_2_ = bf16[544,256]{1,0:T(8,128)(2,1)S(1)} collective-permute-done((bf16[544,256]{1,0:T(8,128)(2,1)S(1)}, bf16[544,256]{1,0:T(8,128)(2,1)S(1)}, u32[]{:S(2)}, u32[]{:S(2)}) %collective-permute-start.6) | collective-permute-done | bytes 278560 | tf_op jit(solution)/shard_map/ppermute | solution.py:354
  57.9 1.1 %merge.2 = bf16[512,384]{1,0:T(8,128)(2,1)S(1)} custom-call(bf16[544,256]{1,0:T(8,128)(2,1)S(1)} %collective-permute-done.2.refs_0_, bf16[544,256]{1,0:T(8,128)(2,1)S(1)} %collective-permute-done.4.refs_1_, bf16[544,256]{1,0:T(8,128)(2,1)S(1)} %collective-permute-done.6.refs_2_, bf16[544,256]{1,0:T(8,128)(2,1)S(1)} %attend.7.refs_3_), custom_call_target="tpu_custom_call" | custom-call | tf_op jit(solution)/shard_map/merge/pallas_call | solution.py:248
  59.0 13.2 %all_to_all.11.refs_0_ = bf16[8,64,384]{2,1,0:T(8,128)(2,1)S(1)} all-to-all(bf16[8,64,384]{2,1,0:T(8,128)(2,1)S(1)} %bitcast.8), channel_id=1, replica_groups=mesh['x'=4,'z'=8,'ylo'=2,'yhi'=2,'core'=2] {'z'}, dimensions={0} | all-to-all | bytes 786432 | tf_op jit(solution)/shard_map/all_to_all | solution.py:380
  72.3 0.4 merge.3
  72.7 1.4 %collective-permute-start.7 = (bf16[32,384]{1,0:T(8,128)(2,1)S(1)}, bf16[32,384]{1,0:T(8,128)(2,1)S(1)}, u32[]{:S(2)}, u32[]{:S(2)}) collective-permute-start(bf16[32,384]{1,0:T(8,128)(2,1)S(1)} %get-tuple-element.20), channel_id=1, source_target_pairs={{0,4},{4,0},{1,5},{5,1},{2,6},{6,2},{3,7},{7,3},{8,12},{12,8},{9,1... | collective-permute-start | bytes 73736 | tf_op jit(solution)/shard_map/ppermute | solution.py:359
  74.1 1.7 %collective-permute-done.7.refs_1_ = bf16[32,384]{1,0:T(8,128)(2,1)S(1)} collective-permute-done((bf16[32,384]{1,0:T(8,128)(2,1)S(1)}, bf16[32,384]{1,0:T(8,128)(2,1)S(1)}, u32[]{:S(2)}, u32[]{:S(2)}) %collective-permute-start.7) | collective-permute-done | bytes 24608 | tf_op jit(solution)/shard_map/ppermute | solution.py:359
  76.0 8.1 %collective-permute-start.8 = (f32[32,512]{1,0:T(8,128)S(1)}, f32[32,512]{1,0:T(8,128)S(1)}, u32[]{:S(2)}, u32[]{:S(2)}) collective-permute-start(f32[32,512]{1,0:T(8,128)S(1)} %dynamic-slice_bitcast_fusion), channel_id=1, source_target_pairs={{0,1},{1,0},{2,3},{3,2},{4,5},{5,4},{6,7},{7,6},{8,9},{9,8},{10,11... | collective-permute-start | bytes 196616 | tf_op jit(solution)/shard_map/ppermute | solution.py:359
  84.2 0.9 collective-permute-done.8.other_ref
  85.1 3.0 %collective-permute-start.9 = (f32[32,512]{1,0:T(8,128)S(1)}, f32[32,512]{1,0:T(8,128)S(1)}, u32[]{:S(2)}, u32[]{:S(2)}) collective-permute-start(f32[32,512]{1,0:T(8,128)S(1)} %pair_sum.1.one_ref), channel_id=1, source_target_pairs={{0,2},{1,3},{2,0},{3,1},{4,6},{5,7},{6,4},{7,5},{8,10},{9,11},{10,... | collective-permute-start | bytes 196616 | tf_op jit(solution)/shard_map/ppermute | solution.py:359
  88.1 1.7 %collective-permute-done.9.two_ref = f32[32,512]{1,0:T(8,128)S(1)} collective-permute-done((f32[32,512]{1,0:T(8,128)S(1)}, f32[32,512]{1,0:T(8,128)S(1)}, u32[]{:S(2)}, u32[]{:S(2)}) %collective-permute-start.9) | collective-permute-done | bytes 65568 | tf_op jit(solution)/shard_map/ppermute | solution.py:359
  89.8 1.6 %collective-permute-start.10 = (bf16[32,512]{1,0:T(8,128)(2,1)S(1)}, bf16[32,512]{1,0:T(8,128)(2,1)S(1)}, u32[]{:S(2)}, u32[]{:S(2)}) collective-permute-start(bf16[32,512]{1,0:T(8,128)(2,1)S(1)} %residual.1.own_ref), channel_id=1, source_target_pairs={{0,1},{1,0},{2,3},{3,2},{4,5},{5,4},{6,7},{7,6},{8,9},{9,8},{10,11... | collective-permute-start | bytes 98312 | tf_op jit(solution)/shard_map/ppermute | solution.py:359
  91.4 0.9 collective-permute-done.10.other_ref
  92.2 2.7 %mlp.1 = (bf16[4,32,256]{2,1,0:T(8,128)(2,1)S(1)}, bf16[2,2,32,256]{3,2,1,0:T(8,128)(2,1)S(1)}) custom-call(s32[1]{0:T(128)} %bitcast.1.core_ref, bf16[32,512]{1,0:T(8,128)(2,1)S(1)} %residual.1.own_ref, bf16[32,512]{1,0:T(8,128)(2,1)S(1)} %collective-permute-done.10.other_ref, bf16[1024,1024]{1,0:T(8,128)(2,1)} %w_up_hbm.1, bf16[1024,1024]{1,0:T(8,128)(2,1)} %w_down_hbm.1), custom_call_target="tpu_custom_call" | custom-call | tf_op jit(solution)/shard_map/mlp/pallas_call | solution.py:324
  95.0 0.4 collective-permute-start.11
  95.5 0.8 collective-permute-done.11.other_ref
  96.3 0.6 pair_shares.1
  96.8 3.0 %collective-permute-start.12 = (f32[32,256]{1,0:T(8,128)S(1)}, f32[32,256]{1,0:T(8,128)S(1)}, u32[]{:S(2)}, u32[]{:S(2)}) collective-permute-start(f32[32,256]{1,0:T(8,128)S(1)} %get-tuple-element.24), channel_id=1, source_target_pairs={{0,2},{1,3},{2,0},{3,1},{4,6},{5,7},{6,4},{7,5},{8,10},{9,11},{10,... | collective-permute-start | bytes 98312 | tf_op jit(solution)/shard_map/ppermute | solution.py:359
  99.9 1.4 %collective-permute-done.12.other_ref = f32[32,256]{1,0:T(8,128)S(1)} collective-permute-done((f32[32,256]{1,0:T(8,128)S(1)}, f32[32,256]{1,0:T(8,128)S(1)}, u32[]{:S(2)}, u32[]{:S(2)}) %collective-permute-start.12) | collective-permute-done | bytes 32800 | tf_op jit(solution)/shard_map/ppermute | solution.py:359
  101.2 1.2 %close.1 = bf16[32,256]{1,0:T(8,128)(2,1)} custom-call(s32[2]{0:T(128)S(1)} %pad_add_fusion.place_ref, bf16[4,32,256]{2,1,0:T(8,128)(2,1)S(1)} %get-tuple-element.21.resid_ref, f32[32,256]{1,0:T(8,128)S(1)} %get-tuple-element.23.kept_ref, f32[32,256]{1,0:T(8,128)S(1)} %collective-permute-done.12.other_ref), custom_call_target="tpu_custom_call" | custom-call | tf_op jit(solution)/shard_map/close/pallas_call | solution.py:276
  (19 shorter events, 1.1 us)
Async XLA Ops:
  1.3 3.3 %collective-permute-start = (bf16[32,256]{1,0:T(8,128)(2,1)S(1)}, bf16[32,256]{1,0:T(8,128)(2,1)S(1)}, u32[]{:S(2)}, u32[]{:S(2)}) collective-permute-start(bf16[32,256]{1,0:T(8,128)(2,1)S(1)} %make_queries.1), channel_id=1, source_target_pairs={{0,4},{4,0},{1,5},{5,1},{2,6},{6,2},{3,7},{7,3},{8,12},{12,8},{9,1... | collective-permute-start | bytes 49160 | tf_op jit(solution)/shard_map/ppermute | solution.py:359
  22.1 11.1 %collective-permute-start.1 = (bf16[512,256]{1,0:T(8,128)(2,1)S(1)}, bf16[512,256]{1,0:T(8,128)(2,1)S(1)}, u32[]{:S(2)}, u32[]{:S(2)}) collective-permute-start(bf16[512,256]{1,0:T(8,128)(2,1)S(1)} %bitcast.9), channel_id=1, source_target_pairs={{0,128},{64,192},{128,0},{192,64},{1,129},{65,193},{129,1},{193,65... | collective-permute-start | bytes 786440 | tf_op jit(solution)/shard_map/ppermute | solution.py:354
  24.8 14.0 %collective-permute-start.3 = (bf16[512,256]{1,0:T(8,128)(2,1)S(1)}, bf16[512,256]{1,0:T(8,128)(2,1)S(1)}, u32[]{:S(2)}, u32[]{:S(2)}) collective-permute-start(bf16[512,256]{1,0:T(8,128)(2,1)S(1)} %bitcast.10), channel_id=1, source_target_pairs={{0,64},{64,128},{128,192},{192,0},{1,65},{65,129},{129,193},{193,1... | collective-permute-start | bytes 786440 | tf_op jit(solution)/shard_map/ppermute | solution.py:354
  25.1 20.6 %collective-permute-start.5 = (bf16[512,256]{1,0:T(8,128)(2,1)S(1)}, bf16[512,256]{1,0:T(8,128)(2,1)S(1)}, u32[]{:S(2)}, u32[]{:S(2)}) collective-permute-start(bf16[512,256]{1,0:T(8,128)(2,1)S(1)} %bitcast.11), channel_id=1, source_target_pairs={{0,192},{64,0},{128,64},{192,128},{1,193},{65,1},{129,65},{193,129... | collective-permute-start | bytes 786440 | tf_op jit(solution)/shard_map/ppermute | solution.py:354
  38.5 18.1 %collective-permute-start.2 = (bf16[544,256]{1,0:T(8,128)(2,1)S(1)}, bf16[544,256]{1,0:T(8,128)(2,1)S(1)}, u32[]{:S(2)}, u32[]{:S(2)}) collective-permute-start(bf16[544,256]{1,0:T(8,128)(2,1)S(1)} %attend.4), channel_id=1, source_target_pairs={{0,128},{64,192},{128,0},{192,64},{1,129},{65,193},{129,1},{193,65... | collective-permute-start | bytes 835592 | tf_op jit(solution)/shard_map/ppermute | solution.py:354
  44.1 12.5 %collective-permute-start.4 = (bf16[544,256]{1,0:T(8,128)(2,1)S(1)}, bf16[544,256]{1,0:T(8,128)(2,1)S(1)}, u32[]{:S(2)}, u32[]{:S(2)}) collective-permute-start(bf16[544,256]{1,0:T(8,128)(2,1)S(1)} %attend.5), channel_id=1, source_target_pairs={{0,192},{64,0},{128,64},{192,128},{1,193},{65,1},{129,65},{193,129... | collective-permute-start | bytes 835592 | tf_op jit(solution)/shard_map/ppermute | solution.py:354
  51.0 6.9 %collective-permute-start.6 = (bf16[544,256]{1,0:T(8,128)(2,1)S(1)}, bf16[544,256]{1,0:T(8,128)(2,1)S(1)}, u32[]{:S(2)}, u32[]{:S(2)}) collective-permute-start(bf16[544,256]{1,0:T(8,128)(2,1)S(1)} %attend.6), channel_id=1, source_target_pairs={{0,64},{64,128},{128,192},{192,0},{1,65},{65,129},{129,193},{193,1... | collective-permute-start | bytes 835592 | tf_op jit(solution)/shard_map/ppermute | solution.py:354
  56.6 19.1 %copy-start = (bf16[256,1024]{1,0:T(8,128)(2,1)S(1)}, bf16[256,1024]{1,0:T(8,128)(2,1)}, u32[]{:S(2)}) copy-start(bf16[256,1024]{1,0:T(8,128)(2,1)} %refs_2_.1) | copy-start | bytes 1572868
  56.6 33.1 %copy-start.1 = (bf16[32,1024]{1,0:T(8,128)(2,1)S(1)}, bf16[32,1024]{1,0:T(8,128)(2,1)}, u32[]{:S(2)}) copy-start(bf16[32,1024]{1,0:T(8,128)(2,1)} %latent_ref.1) | copy-start | bytes 196612
  72.7 3.1 %collective-permute-start.7 = (bf16[32,384]{1,0:T(8,128)(2,1)S(1)}, bf16[32,384]{1,0:T(8,128)(2,1)S(1)}, u32[]{:S(2)}, u32[]{:S(2)}) collective-permute-start(bf16[32,384]{1,0:T(8,128)(2,1)S(1)} %get-tuple-element.20), channel_id=1, source_target_pairs={{0,4},{4,0},{1,5},{5,1},{2,6},{6,2},{3,7},{7,3},{8,12},{12,8},{9,1... | collective-permute-start | bytes 73736 | tf_op jit(solution)/shard_map/ppermute | solution.py:359
  76.0 9.0 %collective-permute-start.8 = (f32[32,512]{1,0:T(8,128)S(1)}, f32[32,512]{1,0:T(8,128)S(1)}, u32[]{:S(2)}, u32[]{:S(2)}) collective-permute-start(f32[32,512]{1,0:T(8,128)S(1)} %dynamic-slice_bitcast_fusion), channel_id=1, source_target_pairs={{0,1},{1,0},{2,3},{3,2},{4,5},{5,4},{6,7},{7,6},{8,9},{9,8},{10,11... | collective-permute-start | bytes 196616 | tf_op jit(solution)/shard_map/ppermute | solution.py:359
  85.1 4.7 %collective-permute-start.9 = (f32[32,512]{1,0:T(8,128)S(1)}, f32[32,512]{1,0:T(8,128)S(1)}, u32[]{:S(2)}, u32[]{:S(2)}) collective-permute-start(f32[32,512]{1,0:T(8,128)S(1)} %pair_sum.1.one_ref), channel_id=1, source_target_pairs={{0,2},{1,3},{2,0},{3,1},{4,6},{5,7},{6,4},{7,5},{8,10},{9,11},{10,... | collective-permute-start | bytes 196616 | tf_op jit(solution)/shard_map/ppermute | solution.py:359
  89.8 2.4 %collective-permute-start.10 = (bf16[32,512]{1,0:T(8,128)(2,1)S(1)}, bf16[32,512]{1,0:T(8,128)(2,1)S(1)}, u32[]{:S(2)}, u32[]{:S(2)}) collective-permute-start(bf16[32,512]{1,0:T(8,128)(2,1)S(1)} %residual.1.own_ref), channel_id=1, source_target_pairs={{0,1},{1,0},{2,3},{3,2},{4,5},{5,4},{6,7},{7,6},{8,9},{9,8},{10,11... | collective-permute-start | bytes 98312 | tf_op jit(solution)/shard_map/ppermute | solution.py:359
  95.0 1.3 %collective-permute-start.11 = (bf16[2,32,256]{2,1,0:T(8,128)(2,1)S(1)}, bf16[2,32,256]{2,1,0:T(8,128)(2,1)S(1)}, u32[]{:S(2)}, u32[]{:S(2)}) collective-permute-start(bf16[2,32,256]{2,1,0:T(8,128)(2,1)S(1)} %dynamic-slice_bitcast_fusion.1), channel_id=1, source_target_pairs={{0,1},{1,0},{2,3},{3,2},{4,5},{5,4},{6,7},{7,6},{8,9},{9,8},{10,11... | collective-permute-start | bytes 98312 | tf_op jit(solution)/shard_map/ppermute | solution.py:359
  96.8 4.4 %collective-permute-start.12 = (f32[32,256]{1,0:T(8,128)S(1)}, f32[32,256]{1,0:T(8,128)S(1)}, u32[]{:S(2)}, u32[]{:S(2)}) collective-permute-start(f32[32,256]{1,0:T(8,128)S(1)} %get-tuple-element.24), channel_id=1, source_target_pairs={{0,2},{1,3},{2,0},{3,1},{4,6},{5,7},{6,4},{7,5},{8,10},{9,11},{10,... | collective-permute-start | bytes 98312 | tf_op jit(solution)/shard_map/ppermute | solution.py:359
where the time goes:
time: 103 us; the launch traced here: 102 us
  Pallas kernels  34.5 us (33%)
  blocking collectives  30.6 us (30%)
  starting transfers between devices  27.3 us (27%)
  waiting for transfers between devices  9.67 us (9%)
    pallas_call x4, Pallas kernels, attend(): pl.pallas_call(functools.partial(attend_kernel, count), out_shape=[jax.Sh...  21.3 us
    ppermute x7, starting transfers between devices, swapped(): return lax.ppermute(value, axes, [(i, i ^ bits) for i in range(size)])  19.7 us
    all_to_all x1, blocking collectives, on_device(): lax.all_to_all(spread, 'z', 0, 0, tiled=True)  17.4 us
    all_to_all x1, blocking collectives, on_device(): lax.all_to_all(block.reshape(count, 2 * rows, -1), 'z', 0, 0, tiled=True)  13.2 us
    ppermute x7, waiting for transfers between devices, swapped(): return lax.ppermute(value, axes, [(i, i ^ bits) for i in range(size)])  8.41 us
    ppermute x6, starting transfers between devices, along(): lax.ppermute(value, axis, [(i, (i + by) % size) for i in range(size)])  7.55 us
    pallas_call x1, Pallas kernels, make_keys_values(): pl.pallas_call(functools.partial(key_value_kernel, block), in_specs=[pl.B...  5.69 us
    pallas_call x1, Pallas kernels, mlp(): pl.pallas_call(mlp_kernel, in_specs=[pl.BlockSpec(memory_space=pltpu.SMEM...  2.71 us
  transfers between devices with their start and end apart: 13, of which 8 were waited for; matrix products, arithmetic and copies ran while one was open for 0% of the time, Pallas kernels for 26%

commit v1 on v0

--- a/solution.py
+++ b/solution.py
@@ -136,9 +136,17 @@
     return rows // (2 * LANES) * LEVEL_ROWS
 
 
-def attend_kernel(count, *refs):
+def attend_kernel(count, fetched, *refs):
     query_refs, (key_ref, value_ref) = refs[:count], refs[count : count + 2]
-    out_refs = refs[count + 2 :]
+    out_refs = refs[count + 2 + fetched :][:count]
+    copies = []
+    if fetched:
+        sems = refs[-1]
+        sources, kept = refs[count + 2 :][:fetched], refs[2 * count + 2 + fetched :][:fetched]
+        for i, (source, target) in enumerate(zip(sources, kept)):
+            copies.append(pltpu.make_async_copy(source, target, sems.at[i]))
+    for copy in copies:
+        copy.start()
     rows = query_refs[0].shape[0]
     total_rows = rows * count
 
@@ -176,17 +184,23 @@
             start = i * rows + j * 2 * LANES
             span = slice(rows + j * LEVEL_ROWS, rows + (j + 1) * LEVEL_ROWS)
             ref[span] = packed[:, start : start + 2 * LANES]
-
-
-def attend(chunks, keys, values):
+    for copy in copies:
+        copy.wait()
+
+
+def attend(chunks, keys, values, fetched=()):
     count = len(chunks)
     rows = chunks[0].shape[0]
-    return pl.pallas_call(
-        functools.partial(attend_kernel, count),
-        out_shape=[jax.ShapeDtypeStruct((rows + level_rows(rows), 2 * LANES), BF16)] * count,
-        compiler_params=params(20),
+    out = jax.ShapeDtypeStruct((rows + level_rows(rows), 2 * LANES), BF16)
+    vmem, hbm = pl.BlockSpec(memory_space=pltpu.VMEM), pl.BlockSpec(memory_space=pltpu.HBM)
+    return pl.pallas_call(
+        functools.partial(attend_kernel, count, len(fetched)),
+        in_specs=[vmem] * (count + 2) + [hbm] * len(fetched),
+        out_shape=[out] * count + [jax.ShapeDtypeStruct(w.shape, BF16) for w in fetched],
+        scratch_shapes=[pltpu.SemaphoreType.DMA((len(fetched),))] if fetched else [],
+        compiler_params=params(24),
         name="attend",
-    )(*chunks, keys, values)
+    )(*chunks, keys, values, *[in_hbm(w) for w in fetched])
 
 
 def spread_matrix(count):
@@ -222,7 +236,7 @@
     return accum / total, highest, total
 
 
-def merge_kernel(count, read, *refs):
+def merge_kernel(count, read, targets, *refs):
     out_refs = refs[count:]
     pieces = [ref[...] for ref in refs[:count]]
     if count == 1:
@@ -237,17 +251,32 @@
         head == 0, one, jnp.where(head == 1, one_other, jnp.where(head == 2, two, two_other))
     )
     packed = split_levels(picked, lane).astype(BF16)
-    rows = out_refs[0].shape[0]
-    for i, ref in enumerate(out_refs):
-        span = slice(i * rows, (i + 1) * rows)
-        ref[:, : 2 * LANES] = mean[span].astype(BF16)
-        ref[:, 2 * LANES :] = packed[span]
-
-
-def merge(pieces, read, rows, parts):
-    return pl.pallas_call(
-        functools.partial(merge_kernel, len(pieces), read),
-        out_shape=[jax.ShapeDtypeStruct((rows // parts, 3 * LANES), BF16)] * parts,
+    mean = mean.astype(BF16)
+    for ref, index, source, rows in targets(out_refs):
+        span = slice(source, source + rows)
+        ref[index + (slice(None, 2 * LANES),)] = mean[span]
+        ref[index + (slice(2 * LANES, None),)] = packed[span]
+
+
+def in_turn(refs):
+    rows = refs[0].shape[0]
+    return [(ref, (slice(None),), i * rows, rows) for i, ref in enumerate(refs)]
+
+
+def side_by_side(refs):
+    count, pair, _ = refs[0].shape
+    rows = pair // 2
+    return [
+        (refs[0], (i, slice(half * rows, (half + 1) * rows)), (half * count + i) * rows, rows)
+        for half in range(2)
+        for i in range(count)
+    ]
+
+
+def merge(pieces, read, targets, shapes):
+    return pl.pallas_call(
+        functools.partial(merge_kernel, len(pieces), read, targets),
+        out_shape=[jax.ShapeDtypeStruct(shape, BF16) for shape in shapes],
         compiler_params=params(24),
         name="merge",
     )(*pieces)
@@ -283,33 +312,29 @@
     )(place, *operands)
 
 
-def add_kernel(core_ref, halves_ref, other_ref, out_ref):
-    out_ref[...] = halves_ref[core_ref[0]] + other_ref[...]
-
-
-def residual_kernel(core_ref, one_ref, two_ref, latent_ref, out_ref):
+def add_kernel(place_ref, halves_ref, other_ref, out_ref):
+    out_ref[...] = halves_ref[place_ref[0] % 2] + other_ref[...]
+
+
+def residual_kernel(place_ref, one_ref, two_ref, latent_ref, out_ref):
     columns = out_ref.shape[1]
-    own = latent_ref[:, pl.ds(pl.multiple_of(core_ref[0] * columns, LANES), columns)]
+    own = latent_ref[:, pl.ds(pl.multiple_of(place_ref[0] % 2 * columns, LANES), columns)]
     out_ref[...] = (own.astype(F32) + (one_ref[...] + two_ref[...])).astype(BF16)
 
 
-def mlp_kernel(core_ref, own_ref, other_ref, w_up_hbm, w_down_hbm, *refs):
-    resid_ref, share_ref, w_up_ref, w_down_ref, sems = refs
-    copies = [
-        pltpu.make_async_copy(w_up_hbm, w_up_ref, sems.at[0]),
-        pltpu.make_async_copy(w_down_hbm, w_down_ref, sems.at[1]),
-    ]
-    for copy in copies:
-        copy.start()
+def mlp_kernel(
+    place_ref, own_ref, other_ref, w_up_ref, w_down_hbm, resid_ref, share_ref, w_down_ref, sem
+):
+    copy = pltpu.make_async_copy(w_down_hbm, w_down_ref, sem)
+    copy.start()
     columns = resid_ref.shape[2]
     own, other = own_ref[...], other_ref[...]
-    low = core_ref[0] == 0
+    low = place_ref[0] % 2 == 0
     residual = jnp.concatenate([jnp.where(low, own, other), jnp.where(low, other, own)], axis=1)
     normed = norm_rows(residual.astype(F32)).astype(BF16)
-    copies[0].wait()
     raised = product(normed, w_up_ref[...])
     hidden = (0.5 * raised * (1.0 + lax.erf(raised * 0.5**0.5))).astype(BF16)
-    copies[1].wait()
+    copy.wait()
     share = product(hidden, w_down_ref[...]).astype(BF16)
     for high in range(2):
         for core in range(2):
@@ -318,34 +343,30 @@
             share_ref[core, high] = share[:, i * columns : (i + 1) * columns]
 
 
-def mlp(core, own, other, w_up, w_down):
+def mlp(place, own, other, w_up, w_down):
     rows, half = own.shape
     vmem, hbm = pl.BlockSpec(memory_space=pltpu.VMEM), pl.BlockSpec(memory_space=pltpu.HBM)
     return pl.pallas_call(
         mlp_kernel,
-        in_specs=[pl.BlockSpec(memory_space=pltpu.SMEM), vmem, vmem, hbm, hbm],
+        in_specs=[pl.BlockSpec(memory_space=pltpu.SMEM), vmem, vmem, vmem, hbm],
         out_shape=[
             jax.ShapeDtypeStruct((4, rows, half // 2), BF16),
             jax.ShapeDtypeStruct((2, 2, rows, half // 2), BF16),
         ],
-        scratch_shapes=[
-            pltpu.VMEM(w_up.shape, BF16),
-            pltpu.VMEM(w_down.shape, BF16),
-            pltpu.SemaphoreType.DMA((2,)),
-        ],
+        scratch_shapes=[pltpu.VMEM(w_down.shape, BF16), pltpu.SemaphoreType.DMA],
         compiler_params=params(16),
         name="mlp",
-    )(core, own, other, in_hbm(w_up), in_hbm(w_down))
+    )(place, own, other, w_up, in_hbm(w_down))
 
 
 def pair_kernel(place_ref, shares_ref, other_ref, kept_ref, sent_ref):
-    high, core = place_ref[0], place_ref[1]
+    high, core = place_ref[0] // 2, place_ref[0] % 2
     for ref, index in ((kept_ref, high), (sent_ref, 1 - high)):
         ref[...] = shares_ref[core, index].astype(F32) + other_ref[index].astype(F32)
 
 
 def close_kernel(place_ref, resid_ref, kept_ref, other_ref, out_ref):
-    own = resid_ref[place_ref[0] * 2 + place_ref[1]]
+    own = resid_ref[place_ref[0]]
     out_ref[...] = (own.astype(F32) + (kept_ref[...] + other_ref[...])).astype(BF16)
 
 
@@ -366,40 +387,40 @@
     queries = make_queries(latent, w_query)
     rows, columns = queries.shape
     count = lax.axis_size("z")
-    both = jnp.concatenate([queries, swapped(queries, "ylo", 1)], axis=0)
-    spread = jnp.broadcast_to(both[None], (count,) + both.shape)
-    part = lax.all_to_all(spread, "z", 0, 0, tiled=True).reshape(count * 2 * rows, columns)
+    spread = jnp.broadcast_to(queries[None], (count,) + queries.shape)
+    part = lax.all_to_all(spread, "z", 0, 0, tiled=True).reshape(count * rows, columns)
+    part = jnp.concatenate([part, swapped(part, "ylo", 1)], axis=0)
     arrived = [along(part, "x", by) for by in STEPS]
     inputs, part = lax.optimization_barrier((inputs, part))
     keys, values = make_keys_values(inputs, w_key, w_value)
     pieces = []
     for by, chunk in zip(STEPS, arrived):
         pieces.append(along(attend([chunk], keys, values)[0], "x", -by))
-    pieces.append(attend([part], keys, values)[0])
-    block = merge(pieces, under_levels, part.shape[0], 1)[0]
-    block = lax.all_to_all(block.reshape(count, 2 * rows, -1), "z", 0, 0, tiled=True)
-    own, others = merge([block], side_levels, 2 * rows, 2)
+    piece, w_up = attend([part], keys, values, (w_up,))
+    pieces.append(piece)
+    block = merge(pieces, under_levels, side_by_side, [(count, 2 * rows, 3 * LANES)])[0]
+    block = lax.all_to_all(block, "z", 0, 0, tiled=True)
+    own, others = merge([block], side_levels, in_turn, [(rows, 3 * LANES)] * 2)
     pieces = [own, swapped(others, "ylo", 1)]
     high, core = lax.axis_index("yhi"), lax.axis_index("core")
-    place = jnp.stack([high, core]).astype(jnp.int32)
-    core_place = place[1:]
+    place = (high * 2 + core).astype(jnp.int32).reshape(1)
     width = latent.shape[1]
     half = jax.ShapeDtypeStruct((rows, width // 2), F32)
     quarter = jax.ShapeDtypeStruct((rows, width // 4), F32)
     halves = project(pieces, w_out)
     other = swapped(lax.dynamic_index_in_dim(halves, 1 - core, 0, keepdims=False), HEAD, 1)
-    pair = placed_call(add_kernel, "pair_sum", half, core_place, halves, other)
+    pair = placed_call(add_kernel, "pair_sum", half, place, halves, other)
     across = swapped(pair, HEAD, 2)
     resid_half = placed_call(
         residual_kernel,
         "residual",
         jax.ShapeDtypeStruct(half.shape, BF16),
-        core_place,
+        place,
         pair,
         across,
         latent,
     )
-    resid, shares = mlp(core_place, resid_half, swapped(resid_half, HEAD, 1), w_up, w_down)
+    resid, shares = mlp(place, resid_half, swapped(resid_half, HEAD, 1), w_up, w_down)
     other = swapped(lax.dynamic_index_in_dim(shares, 1 - core, 0, keepdims=False), HEAD, 1)
     kept, sent = placed_call(pair_kernel, "pair_shares", [quarter] * 2, place, shares, other)
     return placed_call(

time: 103 us -> 101 us (0.981)
  waiting for transfers between devices: 9.67 us -> 11.1 us
  Pallas kernels: 34.5 us -> 33.2 us
    ppermute x7, waiting for transfers between devices: 8.41 us -> 9.87 us  [swapped(): return lax.ppermute(value, axes, [(i, i ^ bits) for i in range(size)])]
    pallas_call x4, Pallas kernels: 1.73 us -> 0.65 us  [placed_call(): pl.pallas_call(kernel, in_specs=[pl.BlockSpec(memory_space=pltpu.SMEM)] +...]
    ppermute x7, starting transfers between devices: 19.7 us -> 18.7 us  [swapped(): return lax.ppermute(value, axes, [(i, i ^ bits) for i in range(size)])]
  transfers between devices with their start and end apart: 13 -> 13, of which waited for: 8 -> 8; matrix products, arithmetic and copies ran while one was open for 0% -> 0% of each run, Pallas kernels for 26% -> 27%
where the time goes in v1:
time: 101 us
  Pallas kernels  33.2 us (33%)
  blocking collectives  29.8 us (30%)
  starting transfers between devices  26.3 us (26%)
  waiting for transfers between devices  11.1 us (11%)
    pallas_call x4, Pallas kernels, attend(): pl.pallas_call(functools.partial(attend_kernel, count, len(fetched)), in_...  21.3 us
    ppermute x7, starting transfers between devices, swapped(): return lax.ppermute(value, axes, [(i, i ^ bits) for i in range(size)])  18.7 us
    all_to_all x1, blocking collectives, on_device(): lax.all_to_all(spread, 'z', 0, 0, tiled=True).reshape(count * rows, columns)  16.6 us
    all_to_all x1, blocking collectives, on_device(): block = lax.all_to_all(block, 'z', 0, 0, tiled=True)  13.2 us
    ppermute x7, waiting for transfers between devices, swapped(): return lax.ppermute(value, axes, [(i, i ^ bits) for i in range(size)])  9.87 us
    ppermute x6, starting transfers between devices, along(): lax.ppermute(value, axis, [(i, (i + by) % size) for i in range(size)])  7.66 us
    pallas_call x1, Pallas kernels, make_keys_values(): pl.pallas_call(functools.partial(key_value_kernel, block), in_specs=[pl.B...  5.68 us
    pallas_call x1, Pallas kernels, mlp(): pl.pallas_call(mlp_kernel, in_specs=[pl.BlockSpec(memory_space=pltpu.SMEM...  2.5 us
  transfers between devices with their start and end apart: 13, of which 8 were waited for; matrix products, arithmetic and copies ran while one was open for 0% of the time, Pallas kernels for 27%

profile of v1, /device:TPU:1, one launch (start us, length us, event | category | flops | bytes accessed | tf_op | source)
XLA Modules:
  0.0 100.7 jit_solution(7223859044670809620)
XLA Ops:
  0.0 1.3 %make_queries.1 = bf16[32,256]{1,0:T(8,128)(2,1)S(1)} custom-call(bf16[32,1024]{1,0:T(8,128)(2,1)} %latent_ref.1, bf16[1024,256]{1,0:T(8,128)(2,1)} %w_hbm.1), custom_call_target="tpu_custom_call" | custom-call | tf_op jit(solution)/shard_map/make_queries/pallas_call | solution.py:58
  1.3 16.6 %all_to_all.10 = bf16[8,32,256]{2,1,0:T(8,128)(2,1)S(1)} all-to-all(bf16[8,32,256]{2,1,0:T(8,128)(2,1)S(1)} %broadcast_in_dim.2), channel_id=1, replica_groups=mesh['x'=4,'z'=8,'ylo'=2,'yhi'=2,'core'=2] {'z'}, dimensions={0} | all-to-all | bytes 262144 | tf_op jit(solution)/shard_map/all_to_all | solution.py:391
  17.9 1.3 %collective-permute-start = (bf16[256,256]{1,0:T(8,128)(2,1)S(1)}, bf16[256,256]{1,0:T(8,128)(2,1)S(1)}, u32[]{:S(2)}, u32[]{:S(2)}) collective-permute-start(bf16[256,256]{1,0:T(8,128)(2,1)S(1)} %bitcast.6), channel_id=1, source_target_pairs={{0,4},{4,0},{1,5},{5,1},{2,6},{6,2},{3,7},{7,3},{8,12},{12,8},{9,1... | collective-permute-start | bytes 393224 | tf_op jit(solution)/shard_map/ppermute | solution.py:380
  19.2 2.5 %collective-permute-done = bf16[256,256]{1,0:T(8,128)(2,1)S(1)} collective-permute-done((bf16[256,256]{1,0:T(8,128)(2,1)S(1)}, bf16[256,256]{1,0:T(8,128)(2,1)S(1)}, u32[]{:S(2)}, u32[]{:S(2)}) %collective-permute-start) | collective-permute-done | bytes 131104 | tf_op jit(solution)/shard_map/ppermute | solution.py:380
  21.7 2.8 %collective-permute-start.1 = (bf16[512,256]{1,0:T(8,128)(2,1)S(1)}, bf16[512,256]{1,0:T(8,128)(2,1)S(1)}, u32[]{:S(2)}, u32[]{:S(2)}) collective-permute-start(bf16[512,256]{1,0:T(8,128)(2,1)S(1)} %pad_maximum_fusion.refs_0_), channel_id=1, source_target_pairs={{0,128},{64,192},{128,0},{192,64},{1,129},{65,193},{129,1},{193,65... | collective-permute-start | bytes 786440 | tf_op jit(solution)/shard_map/ppermute | solution.py:375
  24.6 0.3 collective-permute-start.3
  24.9 2.4 %collective-permute-start.5 = (bf16[512,256]{1,0:T(8,128)(2,1)S(1)}, bf16[512,256]{1,0:T(8,128)(2,1)S(1)}, u32[]{:S(2)}, u32[]{:S(2)}) collective-permute-start(bf16[512,256]{1,0:T(8,128)(2,1)S(1)} %pad_maximum_fusion.refs_0_), channel_id=1, source_target_pairs={{0,192},{64,0},{128,64},{192,128},{1,193},{65,1},{129,65},{193,129... | collective-permute-start | bytes 786440 | tf_op jit(solution)/shard_map/ppermute | solution.py:375
  27.3 5.7 %make_keys_values.1 = (bf16[4,2048,64]{2,1,0:T(8,128)(2,1)S(1)}, bf16[4,2048,128]{2,1,0:T(8,128)(2,1)S(1)}) custom-call(bf16[2048,1024]{1,0:T(8,128)(2,1)} %x_hbm, bf16[1024,256]{1,0:T(8,128)(2,1)} %w_key_hbm.1, bf16[1024,256]{1,0:T(8,128)(2,1)} %w_value_hbm.1), custom_call_target="tpu_custom_call" | custom-call | tf_op jit(solution)/shard_map/make_keys_values/pallas_call | solution.py:108
  33.0 5.3 %attend.4 = bf16[544,256]{1,0:T(8,128)(2,1)S(1)} custom-call(bf16[512,256]{1,0:T(8,128)(2,1)S(1)} %collective-permute-done.1.refs_0_, bf16[4,2048,64]{2,1,0:T(8,128)(2,1)S(1)} %get-tuple-element.18.refs_1_, bf16[4,2048,128]{2,1,0:T(8,128)(2,1)S(1)} %get-tuple-element.19.refs_2_), custom_call_target="tpu_custom_call" | custom-call | tf_op jit(solution)/shard_map/attend/pallas_call | solution.py:196
  38.6 5.3 %attend.5 = bf16[544,256]{1,0:T(8,128)(2,1)S(1)} custom-call(bf16[512,256]{1,0:T(8,128)(2,1)S(1)} %collective-permute-done.3.refs_0_, bf16[4,2048,64]{2,1,0:T(8,128)(2,1)S(1)} %get-tuple-element.18.refs_1_, bf16[4,2048,128]{2,1,0:T(8,128)(2,1)S(1)} %get-tuple-element.19.refs_2_), custom_call_target="tpu_custom_call" | custom-call | tf_op jit(solution)/shard_map/attend/pallas_call | solution.py:196
  43.9 1.5 %collective-permute-start.4 = (bf16[544,256]{1,0:T(8,128)(2,1)S(1)}, bf16[544,256]{1,0:T(8,128)(2,1)S(1)}, u32[]{:S(2)}, u32[]{:S(2)}) collective-permute-start(bf16[544,256]{1,0:T(8,128)(2,1)S(1)} %attend.5), channel_id=1, source_target_pairs={{0,192},{64,0},{128,64},{192,128},{1,193},{65,1},{129,65},{193,129... | collective-permute-start | bytes 835592 | tf_op jit(solution)/shard_map/ppermute | solution.py:375
  45.4 5.3 %attend.6 = bf16[544,256]{1,0:T(8,128)(2,1)S(1)} custom-call(bf16[512,256]{1,0:T(8,128)(2,1)S(1)} %collective-permute-done.5.refs_0_, bf16[4,2048,64]{2,1,0:T(8,128)(2,1)S(1)} %get-tuple-element.18.refs_1_, bf16[4,2048,128]{2,1,0:T(8,128)(2,1)S(1)} %get-tuple-element.19.refs_2_), custom_call_target="tpu_custom_call" | custom-call | tf_op jit(solution)/shard_map/attend/pallas_call | solution.py:196
  50.8 0.3 collective-permute-start.6
  51.1 5.3 %attend.7 = (bf16[544,256]{1,0:T(8,128)(2,1)S(1)}, bf16[1024,1024]{1,0:T(8,128)(2,1)S(1)}) custom-call(bf16[512,256]{1,0:T(8,128)(2,1)S(1)} %pad_maximum_fusion.refs_0_, bf16[4,2048,64]{2,1,0:T(8,128)(2,1)S(1)} %get-tuple-element.18.refs_1_, bf16[4,2048,128]{2,1,0:T(8,128)(2,1)S(1)} %get-tuple-element.19.refs_2_, bf16[1024,1024]{1,0:T(8,128)(2,1)} %refs_3_.1), custom_call_target="tpu_custom_call" | custom-call | tf_op jit(solution)/shard_map/attend/pallas_call | solution.py:196
  56.5 1.2 %collective-permute-done.6.refs_2_ = bf16[544,256]{1,0:T(8,128)(2,1)S(1)} collective-permute-done((bf16[544,256]{1,0:T(8,128)(2,1)S(1)}, bf16[544,256]{1,0:T(8,128)(2,1)S(1)}, u32[]{:S(2)}, u32[]{:S(2)}) %collective-permute-start.6) | collective-permute-done | bytes 278560 | tf_op jit(solution)/shard_map/ppermute | solution.py:375
  57.7 1.1 %merge.2 = bf16[8,64,384]{2,1,0:T(8,128)(2,1)S(1)} custom-call(bf16[544,256]{1,0:T(8,128)(2,1)S(1)} %collective-permute-done.2.refs_0_, bf16[544,256]{1,0:T(8,128)(2,1)S(1)} %collective-permute-done.4.refs_1_, bf16[544,256]{1,0:T(8,128)(2,1)S(1)} %collective-permute-done.6.refs_2_, bf16[544,256]{1,0:T(8,128)(2,1)S(1)} %get-tuple-element.21.refs_3_), custom_call_target="tpu_custom_call" | custom-call | tf_op jit(solution)/shard_map/merge/pallas_call | solution.py:277
  58.8 13.2 %all_to_all.11.refs_0_ = bf16[8,64,384]{2,1,0:T(8,128)(2,1)S(1)} all-to-all(bf16[8,64,384]{2,1,0:T(8,128)(2,1)S(1)} %merge.2), channel_id=1, replica_groups=mesh['x'=4,'z'=8,'ylo'=2,'yhi'=2,'core'=2] {'z'}, dimensions={0} | all-to-all | bytes 786432 | tf_op jit(solution)/shard_map/all_to_all | solution.py:402
  72.0 0.4 merge.3
  72.4 1.4 %collective-permute-start.7 = (bf16[32,384]{1,0:T(8,128)(2,1)S(1)}, bf16[32,384]{1,0:T(8,128)(2,1)S(1)}, u32[]{:S(2)}, u32[]{:S(2)}) collective-permute-start(bf16[32,384]{1,0:T(8,128)(2,1)S(1)} %get-tuple-element.23), channel_id=1, source_target_pairs={{0,4},{4,0},{1,5},{5,1},{2,6},{6,2},{3,7},{7,3},{8,12},{12,8},{9,1... | collective-permute-start | bytes 73736 | tf_op jit(solution)/shard_map/ppermute | solution.py:380
  73.8 1.7 %collective-permute-done.7.refs_1_ = bf16[32,384]{1,0:T(8,128)(2,1)S(1)} collective-permute-done((bf16[32,384]{1,0:T(8,128)(2,1)S(1)}, bf16[32,384]{1,0:T(8,128)(2,1)S(1)}, u32[]{:S(2)}, u32[]{:S(2)}) %collective-permute-start.7) | collective-permute-done | bytes 24608 | tf_op jit(solution)/shard_map/ppermute | solution.py:380
  75.8 7.9 %collective-permute-start.8 = (f32[32,512]{1,0:T(8,128)S(1)}, f32[32,512]{1,0:T(8,128)S(1)}, u32[]{:S(2)}, u32[]{:S(2)}) collective-permute-start(f32[32,512]{1,0:T(8,128)S(1)} %dynamic-slice_bitcast_fusion), channel_id=1, source_target_pairs={{0,1},{1,0},{2,3},{3,2},{4,5},{5,4},{6,7},{7,6},{8,9},{9,8},{10,11... | collective-permute-start | bytes 196616 | tf_op jit(solution)/shard_map/ppermute | solution.py:380
  83.8 0.9 collective-permute-done.8.other_ref
  84.7 3.0 %collective-permute-start.9 = (f32[32,512]{1,0:T(8,128)S(1)}, f32[32,512]{1,0:T(8,128)S(1)}, u32[]{:S(2)}, u32[]{:S(2)}) collective-permute-start(f32[32,512]{1,0:T(8,128)S(1)} %pair_sum.1.one_ref), channel_id=1, source_target_pairs={{0,2},{1,3},{2,0},{3,1},{4,6},{5,7},{6,4},{7,5},{8,10},{9,11},{10,... | collective-permute-start | bytes 196616 | tf_op jit(solution)/shard_map/ppermute | solution.py:380
  87.7 1.7 %collective-permute-done.9.two_ref = f32[32,512]{1,0:T(8,128)S(1)} collective-permute-done((f32[32,512]{1,0:T(8,128)S(1)}, f32[32,512]{1,0:T(8,128)S(1)}, u32[]{:S(2)}, u32[]{:S(2)}) %collective-permute-start.9) | collective-permute-done | bytes 65568 | tf_op jit(solution)/shard_map/ppermute | solution.py:380
  89.4 1.6 %collective-permute-start.10 = (bf16[32,512]{1,0:T(8,128)(2,1)S(1)}, bf16[32,512]{1,0:T(8,128)(2,1)S(1)}, u32[]{:S(2)}, u32[]{:S(2)}) collective-permute-start(bf16[32,512]{1,0:T(8,128)(2,1)S(1)} %residual.1.own_ref), channel_id=1, source_target_pairs={{0,1},{1,0},{2,3},{3,2},{4,5},{5,4},{6,7},{7,6},{8,9},{9,8},{10,11... | collective-permute-start | bytes 98312 | tf_op jit(solution)/shard_map/ppermute | solution.py:380
  91.0 0.9 collective-permute-done.10.other_ref
  91.9 2.5 %mlp.1 = (bf16[4,32,256]{2,1,0:T(8,128)(2,1)S(1)}, bf16[2,2,32,256]{3,2,1,0:T(8,128)(2,1)S(1)}) custom-call(s32[1]{0:T(128)} %bitcast.place_ref, bf16[32,512]{1,0:T(8,128)(2,1)S(1)} %residual.1.own_ref, bf16[32,512]{1,0:T(8,128)(2,1)S(1)} %collective-permute-done.10.other_ref, bf16[1024,1024]{1,0:T(8,128)(2,1)S(1)} %get-tuple-element.24.w_up_ref, ...), custom_call_target="tpu_custom_call" | custom-call | tf_op jit(solution)/shard_map/mlp/pallas_call | solution.py:349
  94.4 0.4 collective-permute-start.11
  94.8 0.9 collective-permute-done.11.other_ref
  95.7 3.0 %collective-permute-start.12 = (f32[32,256]{1,0:T(8,128)S(1)}, f32[32,256]{1,0:T(8,128)S(1)}, u32[]{:S(2)}, u32[]{:S(2)}) collective-permute-start(f32[32,256]{1,0:T(8,128)S(1)} %get-tuple-element.28), channel_id=1, source_target_pairs={{0,2},{1,3},{2,0},{3,1},{4,6},{5,7},{6,4},{7,5},{8,10},{9,11},{10,... | collective-permute-start | bytes 98312 | tf_op jit(solution)/shard_map/ppermute | solution.py:380
  98.7 1.4 %collective-permute-done.12.other_ref = f32[32,256]{1,0:T(8,128)S(1)} collective-permute-done((f32[32,256]{1,0:T(8,128)S(1)}, f32[32,256]{1,0:T(8,128)S(1)}, u32[]{:S(2)}, u32[]{:S(2)}) %collective-permute-start.12) | collective-permute-done | bytes 32800 | tf_op jit(solution)/shard_map/ppermute | solution.py:380
  100.1 0.6 close.1
  (18 shorter events, 0.7 us)
Async XLA Ops:
  17.9 3.8 %collective-permute-start = (bf16[256,256]{1,0:T(8,128)(2,1)S(1)}, bf16[256,256]{1,0:T(8,128)(2,1)S(1)}, u32[]{:S(2)}, u32[]{:S(2)}) collective-permute-start(bf16[256,256]{1,0:T(8,128)(2,1)S(1)} %bitcast.6), channel_id=1, source_target_pairs={{0,4},{4,0},{1,5},{5,1},{2,6},{6,2},{3,7},{7,3},{8,12},{12,8},{9,1... | collective-permute-start | bytes 393224 | tf_op jit(solution)/shard_map/ppermute | solution.py:380
  21.7 11.2 %collective-permute-start.1 = (bf16[512,256]{1,0:T(8,128)(2,1)S(1)}, bf16[512,256]{1,0:T(8,128)(2,1)S(1)}, u32[]{:S(2)}, u32[]{:S(2)}) collective-permute-start(bf16[512,256]{1,0:T(8,128)(2,1)S(1)} %pad_maximum_fusion.refs_0_), channel_id=1, source_target_pairs={{0,128},{64,192},{128,0},{192,64},{1,129},{65,193},{129,1},{193,65... | collective-permute-start | bytes 786440 | tf_op jit(solution)/shard_map/ppermute | solution.py:375
  24.6 14.0 %collective-permute-start.3 = (bf16[512,256]{1,0:T(8,128)(2,1)S(1)}, bf16[512,256]{1,0:T(8,128)(2,1)S(1)}, u32[]{:S(2)}, u32[]{:S(2)}) collective-permute-start(bf16[512,256]{1,0:T(8,128)(2,1)S(1)} %pad_maximum_fusion.refs_0_), channel_id=1, source_target_pairs={{0,64},{64,128},{128,192},{192,0},{1,65},{65,129},{129,193},{193,1... | collective-permute-start | bytes 786440 | tf_op jit(solution)/shard_map/ppermute | solution.py:375
  24.9 20.6 %collective-permute-start.5 = (bf16[512,256]{1,0:T(8,128)(2,1)S(1)}, bf16[512,256]{1,0:T(8,128)(2,1)S(1)}, u32[]{:S(2)}, u32[]{:S(2)}) collective-permute-start(bf16[512,256]{1,0:T(8,128)(2,1)S(1)} %pad_maximum_fusion.refs_0_), channel_id=1, source_target_pairs={{0,192},{64,0},{128,64},{192,128},{1,193},{65,1},{129,65},{193,129... | collective-permute-start | bytes 786440 | tf_op jit(solution)/shard_map/ppermute | solution.py:375
  38.3 18.2 %collective-permute-start.2 = (bf16[544,256]{1,0:T(8,128)(2,1)S(1)}, bf16[544,256]{1,0:T(8,128)(2,1)S(1)}, u32[]{:S(2)}, u32[]{:S(2)}) collective-permute-start(bf16[544,256]{1,0:T(8,128)(2,1)S(1)} %attend.4), channel_id=1, source_target_pairs={{0,128},{64,192},{128,0},{192,64},{1,129},{65,193},{129,1},{193,65... | collective-permute-start | bytes 835592 | tf_op jit(solution)/shard_map/ppermute | solution.py:375
  43.9 12.6 %collective-permute-start.4 = (bf16[544,256]{1,0:T(8,128)(2,1)S(1)}, bf16[544,256]{1,0:T(8,128)(2,1)S(1)}, u32[]{:S(2)}, u32[]{:S(2)}) collective-permute-start(bf16[544,256]{1,0:T(8,128)(2,1)S(1)} %attend.5), channel_id=1, source_target_pairs={{0,192},{64,0},{128,64},{192,128},{1,193},{65,1},{129,65},{193,129... | collective-permute-start | bytes 835592 | tf_op jit(solution)/shard_map/ppermute | solution.py:375
  50.8 6.9 %collective-permute-start.6 = (bf16[544,256]{1,0:T(8,128)(2,1)S(1)}, bf16[544,256]{1,0:T(8,128)(2,1)S(1)}, u32[]{:S(2)}, u32[]{:S(2)}) collective-permute-start(bf16[544,256]{1,0:T(8,128)(2,1)S(1)} %attend.6), channel_id=1, source_target_pairs={{0,64},{64,128},{128,192},{192,0},{1,65},{65,129},{129,193},{193,1... | collective-permute-start | bytes 835592 | tf_op jit(solution)/shard_map/ppermute | solution.py:375
  56.5 19.0 %copy-start = (bf16[256,1024]{1,0:T(8,128)(2,1)S(1)}, bf16[256,1024]{1,0:T(8,128)(2,1)}, u32[]{:S(2)}) copy-start(bf16[256,1024]{1,0:T(8,128)(2,1)} %refs_2_.1) | copy-start | bytes 1572868
  56.5 32.9 %copy-start.1 = (bf16[32,1024]{1,0:T(8,128)(2,1)S(1)}, bf16[32,1024]{1,0:T(8,128)(2,1)}, u32[]{:S(2)}) copy-start(bf16[32,1024]{1,0:T(8,128)(2,1)} %latent_ref.1) | copy-start | bytes 196612
  72.4 3.1 %collective-permute-start.7 = (bf16[32,384]{1,0:T(8,128)(2,1)S(1)}, bf16[32,384]{1,0:T(8,128)(2,1)S(1)}, u32[]{:S(2)}, u32[]{:S(2)}) collective-permute-start(bf16[32,384]{1,0:T(8,128)(2,1)S(1)} %get-tuple-element.23), channel_id=1, source_target_pairs={{0,4},{4,0},{1,5},{5,1},{2,6},{6,2},{3,7},{7,3},{8,12},{12,8},{9,1... | collective-permute-start | bytes 73736 | tf_op jit(solution)/shard_map/ppermute | solution.py:380
  75.8 8.9 %collective-permute-start.8 = (f32[32,512]{1,0:T(8,128)S(1)}, f32[32,512]{1,0:T(8,128)S(1)}, u32[]{:S(2)}, u32[]{:S(2)}) collective-permute-start(f32[32,512]{1,0:T(8,128)S(1)} %dynamic-slice_bitcast_fusion), channel_id=1, source_target_pairs={{0,1},{1,0},{2,3},{3,2},{4,5},{5,4},{6,7},{7,6},{8,9},{9,8},{10,11... | collective-permute-start | bytes 196616 | tf_op jit(solution)/shard_map/ppermute | solution.py:380
  84.7 4.7 %collective-permute-start.9 = (f32[32,512]{1,0:T(8,128)S(1)}, f32[32,512]{1,0:T(8,128)S(1)}, u32[]{:S(2)}, u32[]{:S(2)}) collective-permute-start(f32[32,512]{1,0:T(8,128)S(1)} %pair_sum.1.one_ref), channel_id=1, source_target_pairs={{0,2},{1,3},{2,0},{3,1},{4,6},{5,7},{6,4},{7,5},{8,10},{9,11},{10,... | collective-permute-start | bytes 196616 | tf_op jit(solution)/shard_map/ppermute | solution.py:380
  89.4 2.4 %collective-permute-start.10 = (bf16[32,512]{1,0:T(8,128)(2,1)S(1)}, bf16[32,512]{1,0:T(8,128)(2,1)S(1)}, u32[]{:S(2)}, u32[]{:S(2)}) collective-permute-start(bf16[32,512]{1,0:T(8,128)(2,1)S(1)} %residual.1.own_ref), channel_id=1, source_target_pairs={{0,1},{1,0},{2,3},{3,2},{4,5},{5,4},{6,7},{7,6},{8,9},{9,8},{10,11... | collective-permute-start | bytes 98312 | tf_op jit(solution)/shard_map/ppermute | solution.py:380
  94.4 1.3 %collective-permute-start.11 = (bf16[2,32,256]{2,1,0:T(8,128)(2,1)S(1)}, bf16[2,32,256]{2,1,0:T(8,128)(2,1)S(1)}, u32[]{:S(2)}, u32[]{:S(2)}) collective-permute-start(bf16[2,32,256]{2,1,0:T(8,128)(2,1)S(1)} %dynamic-slice_bitcast_fusion.1), channel_id=1, source_target_pairs={{0,1},{1,0},{2,3},{3,2},{4,5},{5,4},{6,7},{7,6},{8,9},{9,8},{10,11... | collective-permute-start | bytes 98312 | tf_op jit(solution)/shard_map/ppermute | solution.py:380
  95.7 4.4 %collective-permute-start.12 = (f32[32,256]{1,0:T(8,128)S(1)}, f32[32,256]{1,0:T(8,128)S(1)}, u32[]{:S(2)}, u32[]{:S(2)}) collective-permute-start(f32[32,256]{1,0:T(8,128)S(1)} %get-tuple-element.28), channel_id=1, source_target_pairs={{0,2},{1,3},{2,0},{3,1},{4,6},{5,7},{6,4},{7,5},{8,10},{9,11},{10,... | collective-permute-start | bytes 98312 | tf_op jit(solution)/shard_map/ppermute | solution.py:380

commit v2 on v1

--- a/solution.py
+++ b/solution.py
@@ -86,12 +86,15 @@
         copy.start()
     lane = lax.broadcasted_iota(jnp.int32, (block, LANES), 1)
     low = lane < HEAD_DIM
+    copies[0].wait()
+    following = norm_rows(x_ref[spans[0]].astype(F32)).astype(BF16)
+    weights[0].wait()
+    weights[1].wait()
     for i, span in enumerate(spans):
-        copies[i].wait()
-        normed = norm_rows(x_ref[span].astype(F32)).astype(BF16)
-        if i == 0:
-            weights[0].wait()
-            weights[1].wait()
+        normed = following
+        if i + 1 < len(spans):
+            copies[i + 1].wait()
+            following = norm_rows(x_ref[spans[i + 1]].astype(F32)).astype(BF16)
         keys = product(normed, w_key_ref[...]).astype(BF16)
         vals = product(normed, w_value_ref[...])
         for head in range(HEADS_HERE):
@@ -236,12 +239,9 @@
     return accum / total, highest, total
 
 
-def merge_kernel(count, read, targets, *refs):
+def merge_kernel(count, write, *refs):
     out_refs = refs[count:]
-    pieces = [ref[...] for ref in refs[:count]]
-    if count == 1:
-        pieces = [pieces[0][i] for i in range(pieces[0].shape[0])]
-    mean, highest, total = merged(pieces, read)
+    mean, highest, total = merged([ref[...] for ref in refs[:count]], under_levels)
     levels = highest + jnp.log(total)
     lane = lax.broadcasted_iota(jnp.int32, (levels.shape[0], LANES), 1)
     one, two = levels[:, :LANES], levels[:, LANES:]
@@ -250,55 +250,35 @@
     picked = jnp.where(
         head == 0, one, jnp.where(head == 1, one_other, jnp.where(head == 2, two, two_other))
     )
-    packed = split_levels(picked, lane).astype(BF16)
-    mean = mean.astype(BF16)
-    for ref, index, source, rows in targets(out_refs):
-        span = slice(source, source + rows)
-        ref[index + (slice(None, 2 * LANES),)] = mean[span]
-        ref[index + (slice(2 * LANES, None),)] = packed[span]
-
-
-def in_turn(refs):
-    rows = refs[0].shape[0]
-    return [(ref, (slice(None),), i * rows, rows) for i, ref in enumerate(refs)]
-
-
-def side_by_side(refs):
-    count, pair, _ = refs[0].shape
-    rows = pair // 2
-    return [
-        (refs[0], (i, slice(half * rows, (half + 1) * rows)), (half * count + i) * rows, rows)
-        for half in range(2)
-        for i in range(count)
-    ]
-
-
-def merge(pieces, read, targets, shapes):
-    return pl.pallas_call(
-        functools.partial(merge_kernel, len(pieces), read, targets),
+    write(out_refs, mean.astype(BF16), split_levels(picked, lane))
+
+
+def write_halves(refs, mean, parts):
+    rows = mean.shape[0] // len(refs)
+    turned = jnp.transpose(parts)[:LEVEL_ROWS].astype(BF16)
+    for i, ref in enumerate(refs):
+        ref[:rows] = mean[i * rows : (i + 1) * rows]
+        for j in range(rows // (2 * LANES)):
+            start = i * rows + j * 2 * LANES
+            span = slice(rows + j * LEVEL_ROWS, rows + (j + 1) * LEVEL_ROWS)
+            ref[span] = turned[:, start : start + 2 * LANES]
+
+
+def write_blocks(refs, mean, parts):
+    count, rows, _ = refs[0].shape
+    parts = parts.astype(BF16)
+    for i in range(count):
+        refs[0][i, :, : 2 * LANES] = mean[i * rows : (i + 1) * rows]
+        refs[0][i, :, 2 * LANES :] = parts[i * rows : (i + 1) * rows]
+
+
+def merge(pieces, write, shapes):
+    return pl.pallas_call(
+        functools.partial(merge_kernel, len(pieces), write),
         out_shape=[jax.ShapeDtypeStruct(shape, BF16) for shape in shapes],
         compiler_params=params(24),
         name="merge",
     )(*pieces)
-
-
-def project_kernel(count, *refs):
-    w_ref, out_ref = refs[count:]
-    mean, highest, total = merged([ref[...] for ref in refs[:count]], side_levels)
-    projected = product(mean.astype(BF16), w_ref[...])
-    columns = out_ref.shape[2]
-    for i in range(out_ref.shape[0]):
-        out_ref[i] = projected[:, i * columns : (i + 1) * columns]
-
-
-def project(pieces, w_out):
-    rows, width = pieces[0].shape[0], w_out.shape[1]
-    return pl.pallas_call(
-        functools.partial(project_kernel, len(pieces)),
-        out_shape=jax.ShapeDtypeStruct((2, rows, width // 2), F32),
-        compiler_params=params(8),
-        name="project",
-    )(*pieces, w_out)
 
 
 def placed_call(kernel, name, out_shape, place, *operands):
@@ -312,8 +292,22 @@
     )(place, *operands)
 
 
-def add_kernel(place_ref, halves_ref, other_ref, out_ref):
-    out_ref[...] = halves_ref[place_ref[0] % 2] + other_ref[...]
+def ordered(place_ref, low, high):
+    first = place_ref[0] % 2 == 0
+    return jnp.where(first, low, high), jnp.where(first, high, low)
+
+
+def project_kernel(place_ref, pieces_ref, w_ref, kept_ref, sent_ref):
+    pieces = [pieces_ref[i] for i in range(pieces_ref.shape[0])]
+    mean, highest, total = merged(pieces, side_levels)
+    projected = product(mean.astype(BF16), w_ref[...])
+    columns = kept_ref.shape[1]
+    halves = ordered(place_ref, projected[:, :columns], projected[:, columns:])
+    kept_ref[...], sent_ref[...] = halves
+
+
+def add_kernel(place_ref, kept_ref, other_ref, out_ref):
+    out_ref[...] = kept_ref[...] + other_ref[...]
 
 
 def residual_kernel(place_ref, one_ref, two_ref, latent_ref, out_ref):
@@ -323,24 +317,33 @@
 
 
 def mlp_kernel(
-    place_ref, own_ref, other_ref, w_up_ref, w_down_hbm, resid_ref, share_ref, w_down_ref, sem
+    place_ref,
+    own_ref,
+    other_ref,
+    w_up_ref,
+    w_down_hbm,
+    resid_ref,
+    kept_ref,
+    sent_ref,
+    w_down_ref,
+    sem,
 ):
     copy = pltpu.make_async_copy(w_down_hbm, w_down_ref, sem)
     copy.start()
     columns = resid_ref.shape[2]
-    own, other = own_ref[...], other_ref[...]
-    low = place_ref[0] % 2 == 0
-    residual = jnp.concatenate([jnp.where(low, own, other), jnp.where(low, other, own)], axis=1)
+    halves = ordered(place_ref, own_ref[...], other_ref[...])
+    residual = jnp.concatenate(halves, axis=1)
     normed = norm_rows(residual.astype(F32)).astype(BF16)
     raised = product(normed, w_up_ref[...])
     hidden = (0.5 * raised * (1.0 + lax.erf(raised * 0.5**0.5))).astype(BF16)
     copy.wait()
     share = product(hidden, w_down_ref[...]).astype(BF16)
+    blocks = [share[:, i * columns : (i + 1) * columns] for i in range(4)]
+    for i in range(4):
+        resid_ref[i] = residual[:, i * columns : (i + 1) * columns]
     for high in range(2):
-        for core in range(2):
-            i = high * 2 + core
-            resid_ref[i] = residual[:, i * columns : (i + 1) * columns]
-            share_ref[core, high] = share[:, i * columns : (i + 1) * columns]
+        pair = ordered(place_ref, blocks[2 * high], blocks[2 * high + 1])
+        kept_ref[high], sent_ref[high] = pair
 
 
 def mlp(place, own, other, w_up, w_down):
@@ -351,8 +354,8 @@
         in_specs=[pl.BlockSpec(memory_space=pltpu.SMEM), vmem, vmem, vmem, hbm],
         out_shape=[
             jax.ShapeDtypeStruct((4, rows, half // 2), BF16),
-            jax.ShapeDtypeStruct((2, 2, rows, half // 2), BF16),
-        ],
+        ]
+        + [jax.ShapeDtypeStruct((2, rows, half // 2), BF16)] * 2,
         scratch_shapes=[pltpu.VMEM(w_down.shape, BF16), pltpu.SemaphoreType.DMA],
         compiler_params=params(16),
         name="mlp",
@@ -360,9 +363,9 @@
 
 
 def pair_kernel(place_ref, shares_ref, other_ref, kept_ref, sent_ref):
-    high, core = place_ref[0] // 2, place_ref[0] % 2
+    high = place_ref[0] // 2
     for ref, index in ((kept_ref, high), (sent_ref, 1 - high)):
-        ref[...] = shares_ref[core, index].astype(F32) + other_ref[index].astype(F32)
+        ref[...] = shares_ref[index].astype(F32) + other_ref[index].astype(F32)
 
 
 def close_kernel(place_ref, resid_ref, kept_ref, other_ref, out_ref):
@@ -398,18 +401,18 @@
         pieces.append(along(attend([chunk], keys, values)[0], "x", -by))
     piece, w_up = attend([part], keys, values, (w_up,))
     pieces.append(piece)
-    block = merge(pieces, under_levels, side_by_side, [(count, 2 * rows, 3 * LANES)])[0]
-    block = lax.all_to_all(block, "z", 0, 0, tiled=True)
-    own, others = merge([block], side_levels, in_turn, [(rows, 3 * LANES)] * 2)
-    pieces = [own, swapped(others, "ylo", 1)]
-    high, core = lax.axis_index("yhi"), lax.axis_index("core")
-    place = (high * 2 + core).astype(jnp.int32).reshape(1)
+    half = (count * rows + level_rows(count * rows), columns)
+    own, others = merge(pieces, write_halves, [half] * 2)
+    block = merge([own, swapped(others, "ylo", 1)], write_blocks, [(count, rows, 3 * LANES)])[0]
+    place = lax.axis_index(HEAD).astype(jnp.int32).reshape(1)
+    block, place = lax.optimization_barrier((block, place))
+    pieces = lax.all_to_all(block, "z", 0, 0, tiled=True)
     width = latent.shape[1]
     half = jax.ShapeDtypeStruct((rows, width // 2), F32)
     quarter = jax.ShapeDtypeStruct((rows, width // 4), F32)
-    halves = project(pieces, w_out)
-    other = swapped(lax.dynamic_index_in_dim(halves, 1 - core, 0, keepdims=False), HEAD, 1)
-    pair = placed_call(add_kernel, "pair_sum", half, place, halves, other)
+    kept, sent = placed_call(project_kernel, "project", [half] * 2, place, pieces, w_out)
+    other = swapped(sent, HEAD, 1)
+    pair = placed_call(add_kernel, "pair_sum", half, place, kept, other)
     across = swapped(pair, HEAD, 2)
     resid_half = placed_call(
         residual_kernel,
@@ -420,9 +423,9 @@
         across,
         latent,
     )
-    resid, shares = mlp(place, resid_half, swapped(resid_half, HEAD, 1), w_up, w_down)
-    other = swapped(lax.dynamic_index_in_dim(shares, 1 - core, 0, keepdims=False), HEAD, 1)
-    kept, sent = placed_call(pair_kernel, "pair_shares", [quarter] * 2, place, shares, other)
+    resid, kept, sent = mlp(place, resid_half, swapped(resid_half, HEAD, 1), w_up, w_down)
+    other = swapped(sent, HEAD, 1)
+    kept, sent = placed_call(pair_kernel, "pair_shares", [quarter] * 2, place, kept, other)
     return placed_call(
         close_kernel,
         "close",

time: 101 us -> 100 us (0.990)
  blocking collectives: 29.8 us -> 27.6 us
  waiting for transfers between devices: 11.1 us -> 12.3 us
    all_to_all x1, blocking collectives: 13.2 us -> 11 us  [on_device(): pieces = lax.all_to_all(block, 'z', 0, 0, tiled=True)]
    ppermute x7, waiting for transfers between devices: 9.87 us -> 11.1 us  [swapped(): return lax.ppermute(value, axes, [(i, i ^ bits) for i in range(size)])]
where the time goes in v2:
time: 100 us; the launch traced here: 99.8 us
  Pallas kernels  33.2 us (33%)
  blocking collectives  27.6 us (28%)
  starting transfers between devices  26.5 us (26%)
  waiting for transfers between devices  12.3 us (12%)
    pallas_call x4, Pallas kernels, attend(): pl.pallas_call(functools.partial(attend_kernel, count, len(fetched)), in_...  21.3 us
    ppermute x7, starting transfers between devices, swapped(): return lax.ppermute(value, axes, [(i, i ^ bits) for i in range(size)])  18.8 us
    all_to_all x1, blocking collectives, on_device(): lax.all_to_all(spread, 'z', 0, 0, tiled=True).reshape(count * rows, columns)  16.6 us
    ppermute x7, waiting for transfers between devices, swapped(): return lax.ppermute(value, axes, [(i, i ^ bits) for i in range(size)])  11.1 us
    all_to_all x1, blocking collectives, on_device(): pieces = lax.all_to_all(block, 'z', 0, 0, tiled=True)  11 us
    ppermute x6, starting transfers between devices, along(): lax.ppermute(value, axis, [(i, (i + by) % size) for i in range(size)])  7.64 us
    pallas_call x1, Pallas kernels, make_keys_values(): pl.pallas_call(functools.partial(key_value_kernel, block), in_specs=[pl.B...  5.51 us
    pallas_call x1, Pallas kernels, mlp(): pl.pallas_call(mlp_kernel, in_specs=[pl.BlockSpec(memory_space=pltpu.SMEM...  2.5 us
  transfers between devices with their start and end apart: 13, of which 8 were waited for; matrix products, arithmetic and copies ran while one was open for 0% of the time, Pallas kernels for 27%

profile of v2, /device:TPU:1, one launch (start us, length us, event | category | flops | bytes accessed | tf_op | source)
XLA Modules:
  0.0 99.8 jit_solution(17379618241015197263)
XLA Ops:
  0.0 1.3 %make_queries.1 = bf16[32,256]{1,0:T(8,128)(2,1)S(1)} custom-call(bf16[32,1024]{1,0:T(8,128)(2,1)} %latent_ref.1, bf16[1024,256]{1,0:T(8,128)(2,1)} %w_hbm.1), custom_call_target="tpu_custom_call" | custom-call | tf_op jit(solution)/shard_map/make_queries/pallas_call | solution.py:58
  1.3 16.6 %all_to_all.10 = bf16[8,32,256]{2,1,0:T(8,128)(2,1)S(1)} all-to-all(bf16[8,32,256]{2,1,0:T(8,128)(2,1)S(1)} %broadcast_in_dim.2), channel_id=1, replica_groups=mesh['x'=4,'z'=8,'ylo'=2,'yhi'=2,'core'=2] {'z'}, dimensions={0} | all-to-all | bytes 262144 | tf_op jit(solution)/shard_map/all_to_all | solution.py:394
  17.9 1.3 %collective-permute-start = (bf16[256,256]{1,0:T(8,128)(2,1)S(1)}, bf16[256,256]{1,0:T(8,128)(2,1)S(1)}, u32[]{:S(2)}, u32[]{:S(2)}) collective-permute-start(bf16[256,256]{1,0:T(8,128)(2,1)S(1)} %bitcast.2), channel_id=1, source_target_pairs={{0,4},{4,0},{1,5},{5,1},{2,6},{6,2},{3,7},{7,3},{8,12},{12,8},{9,1... | collective-permute-start | bytes 393224 | tf_op jit(solution)/shard_map/ppermute | solution.py:383
  19.2 2.5 %collective-permute-done = bf16[256,256]{1,0:T(8,128)(2,1)S(1)} collective-permute-done((bf16[256,256]{1,0:T(8,128)(2,1)S(1)}, bf16[256,256]{1,0:T(8,128)(2,1)S(1)}, u32[]{:S(2)}, u32[]{:S(2)}) %collective-permute-start) | collective-permute-done | bytes 131104 | tf_op jit(solution)/shard_map/ppermute | solution.py:383
  21.7 2.8 %collective-permute-start.1 = (bf16[512,256]{1,0:T(8,128)(2,1)S(1)}, bf16[512,256]{1,0:T(8,128)(2,1)S(1)}, u32[]{:S(2)}, u32[]{:S(2)}) collective-permute-start(bf16[512,256]{1,0:T(8,128)(2,1)S(1)} %pad_maximum_fusion.refs_0_), channel_id=1, source_target_pairs={{0,128},{64,192},{128,0},{192,64},{1,129},{65,193},{129,1},{193,65... | collective-permute-start | bytes 786440 | tf_op jit(solution)/shard_map/ppermute | solution.py:378
  24.9 2.4 %collective-permute-start.5 = (bf16[512,256]{1,0:T(8,128)(2,1)S(1)}, bf16[512,256]{1,0:T(8,128)(2,1)S(1)}, u32[]{:S(2)}, u32[]{:S(2)}) collective-permute-start(bf16[512,256]{1,0:T(8,128)(2,1)S(1)} %pad_maximum_fusion.refs_0_), channel_id=1, source_target_pairs={{0,192},{64,0},{128,64},{192,128},{1,193},{65,1},{129,65},{193,129... | collective-permute-start | bytes 786440 | tf_op jit(solution)/shard_map/ppermute | solution.py:378
  27.3 5.5 %make_keys_values.1 = (bf16[4,2048,64]{2,1,0:T(8,128)(2,1)S(1)}, bf16[4,2048,128]{2,1,0:T(8,128)(2,1)S(1)}) custom-call(bf16[2048,1024]{1,0:T(8,128)(2,1)} %x_hbm, bf16[1024,256]{1,0:T(8,128)(2,1)} %w_key_hbm.1, bf16[1024,256]{1,0:T(8,128)(2,1)} %w_value_hbm.1), custom_call_target="tpu_custom_call" | custom-call | tf_op jit(solution)/shard_map/make_keys_values/pallas_call | solution.py:111
  32.8 5.3 %attend.4 = bf16[544,256]{1,0:T(8,128)(2,1)S(1)} custom-call(bf16[512,256]{1,0:T(8,128)(2,1)S(1)} %collective-permute-done.1.refs_0_, bf16[4,2048,64]{2,1,0:T(8,128)(2,1)S(1)} %get-tuple-element.23.refs_1_, bf16[4,2048,128]{2,1,0:T(8,128)(2,1)S(1)} %get-tuple-element.24.refs_2_), custom_call_target="tpu_custom_call" | custom-call | tf_op jit(solution)/shard_map/attend/pallas_call | solution.py:199
  38.4 5.3 %attend.5 = bf16[544,256]{1,0:T(8,128)(2,1)S(1)} custom-call(bf16[512,256]{1,0:T(8,128)(2,1)S(1)} %collective-permute-done.3.refs_0_, bf16[4,2048,64]{2,1,0:T(8,128)(2,1)S(1)} %get-tuple-element.23.refs_1_, bf16[4,2048,128]{2,1,0:T(8,128)(2,1)S(1)} %get-tuple-element.24.refs_2_), custom_call_target="tpu_custom_call" | custom-call | tf_op jit(solution)/shard_map/attend/pallas_call | solution.py:199
  43.7 1.5 %collective-permute-start.4 = (bf16[544,256]{1,0:T(8,128)(2,1)S(1)}, bf16[544,256]{1,0:T(8,128)(2,1)S(1)}, u32[]{:S(2)}, u32[]{:S(2)}) collective-permute-start(bf16[544,256]{1,0:T(8,128)(2,1)S(1)} %attend.5), channel_id=1, source_target_pairs={{0,192},{64,0},{128,64},{192,128},{1,193},{65,1},{129,65},{193,129... | collective-permute-start | bytes 835592 | tf_op jit(solution)/shard_map/ppermute | solution.py:378
  45.3 5.3 %attend.6 = bf16[544,256]{1,0:T(8,128)(2,1)S(1)} custom-call(bf16[512,256]{1,0:T(8,128)(2,1)S(1)} %collective-permute-done.5.refs_0_, bf16[4,2048,64]{2,1,0:T(8,128)(2,1)S(1)} %get-tuple-element.23.refs_1_, bf16[4,2048,128]{2,1,0:T(8,128)(2,1)S(1)} %get-tuple-element.24.refs_2_), custom_call_target="tpu_custom_call" | custom-call | tf_op jit(solution)/shard_map/attend/pallas_call | solution.py:199
  50.6 0.3 collective-permute-start.6
  50.9 5.3 %attend.7 = (bf16[544,256]{1,0:T(8,128)(2,1)S(1)}, bf16[1024,1024]{1,0:T(8,128)(2,1)S(1)}) custom-call(bf16[512,256]{1,0:T(8,128)(2,1)S(1)} %pad_maximum_fusion.refs_0_, bf16[4,2048,64]{2,1,0:T(8,128)(2,1)S(1)} %get-tuple-element.23.refs_1_, bf16[4,2048,128]{2,1,0:T(8,128)(2,1)S(1)} %get-tuple-element.24.refs_2_, bf16[1024,1024]{1,0:T(8,128)(2,1)} %refs_3_.1), custom_call_target="tpu_custom_call" | custom-call | tf_op jit(solution)/shard_map/attend/pallas_call | solution.py:199
  56.3 1.2 %collective-permute-done.6.refs_2_ = bf16[544,256]{1,0:T(8,128)(2,1)S(1)} collective-permute-done((bf16[544,256]{1,0:T(8,128)(2,1)S(1)}, bf16[544,256]{1,0:T(8,128)(2,1)S(1)}, u32[]{:S(2)}, u32[]{:S(2)}) %collective-permute-start.6) | collective-permute-done | bytes 278560 | tf_op jit(solution)/shard_map/ppermute | solution.py:378
  57.5 1.1 %merge.2 = (bf16[272,256]{1,0:T(8,128)(2,1)S(1)}, bf16[272,256]{1,0:T(8,128)(2,1)S(1)}) custom-call(bf16[544,256]{1,0:T(8,128)(2,1)S(1)} %collective-permute-done.2.refs_0_, bf16[544,256]{1,0:T(8,128)(2,1)S(1)} %collective-permute-done.4.refs_1_, bf16[544,256]{1,0:T(8,128)(2,1)S(1)} %collective-permute-done.6.refs_2_, ...), custom_call_target="tpu_custom_call" | custom-call | tf_op jit(solution)/shard_map/merge/pallas_call | solution.py:276
  58.7 1.4 %collective-permute-start.7 = (bf16[272,256]{1,0:T(8,128)(2,1)S(1)}, bf16[272,256]{1,0:T(8,128)(2,1)S(1)}, u32[]{:S(2)}, u32[]{:S(2)}) collective-permute-start(bf16[272,256]{1,0:T(8,128)(2,1)S(1)} %get-tuple-element.28), channel_id=1, source_target_pairs={{0,4},{4,0},{1,5},{5,1},{2,6},{6,2},{3,7},{7,3},{8,12},{12,8},{9,1... | collective-permute-start | bytes 417800 | tf_op jit(solution)/shard_map/ppermute | solution.py:383
  60.0 2.9 %collective-permute-done.7.refs_1_ = bf16[272,256]{1,0:T(8,128)(2,1)S(1)} collective-permute-done((bf16[272,256]{1,0:T(8,128)(2,1)S(1)}, bf16[272,256]{1,0:T(8,128)(2,1)S(1)}, u32[]{:S(2)}, u32[]{:S(2)}) %collective-permute-start.7) | collective-permute-done | bytes 139296 | tf_op jit(solution)/shard_map/ppermute | solution.py:383
  62.9 0.4 merge.3
  63.4 11.0 %all_to_all.11.pieces_ref = bf16[8,32,384]{2,1,0:T(8,128)(2,1)S(1)} all-to-all(bf16[8,32,384]{2,1,0:T(8,128)(2,1)S(1)} %merge.3), channel_id=1, replica_groups=mesh['x'=4,'z'=8,'ylo'=2,'yhi'=2,'core'=2] {'z'}, dimensions={0} | all-to-all | bytes 393216 | tf_op jit(solution)/shard_map/all_to_all | solution.py:409
  74.4 0.4 project.1
  74.8 8.1 %collective-permute-start.8 = (f32[32,512]{1,0:T(8,128)S(1)}, f32[32,512]{1,0:T(8,128)S(1)}, u32[]{:S(2)}, u32[]{:S(2)}) collective-permute-start(f32[32,512]{1,0:T(8,128)S(1)} %get-tuple-element.32), channel_id=1, source_target_pairs={{0,1},{1,0},{2,3},{3,2},{4,5},{5,4},{6,7},{7,6},{8,9},{9,8},{10,11... | collective-permute-start | bytes 196616 | tf_op jit(solution)/shard_map/ppermute | solution.py:383
  82.9 0.9 collective-permute-done.8.other_ref
  83.8 3.0 %collective-permute-start.9 = (f32[32,512]{1,0:T(8,128)S(1)}, f32[32,512]{1,0:T(8,128)S(1)}, u32[]{:S(2)}, u32[]{:S(2)}) collective-permute-start(f32[32,512]{1,0:T(8,128)S(1)} %pair_sum.1.one_ref), channel_id=1, source_target_pairs={{0,2},{1,3},{2,0},{3,1},{4,6},{5,7},{6,4},{7,5},{8,10},{9,11},{10,... | collective-permute-start | bytes 196616 | tf_op jit(solution)/shard_map/ppermute | solution.py:383
  86.8 1.7 %collective-permute-done.9.two_ref = f32[32,512]{1,0:T(8,128)S(1)} collective-permute-done((f32[32,512]{1,0:T(8,128)S(1)}, f32[32,512]{1,0:T(8,128)S(1)}, u32[]{:S(2)}, u32[]{:S(2)}) %collective-permute-start.9) | collective-permute-done | bytes 65568 | tf_op jit(solution)/shard_map/ppermute | solution.py:383
  88.5 1.6 %collective-permute-start.10 = (bf16[32,512]{1,0:T(8,128)(2,1)S(1)}, bf16[32,512]{1,0:T(8,128)(2,1)S(1)}, u32[]{:S(2)}, u32[]{:S(2)}) collective-permute-start(bf16[32,512]{1,0:T(8,128)(2,1)S(1)} %residual.1.own_ref), channel_id=1, source_target_pairs={{0,1},{1,0},{2,3},{3,2},{4,5},{5,4},{6,7},{7,6},{8,9},{9,8},{10,11... | collective-permute-start | bytes 98312 | tf_op jit(solution)/shard_map/ppermute | solution.py:383
  90.1 0.9 collective-permute-done.10.other_ref
  91.0 2.5 %mlp.1 = (bf16[4,32,256]{2,1,0:T(8,128)(2,1)S(1)}, bf16[2,32,256]{2,1,0:T(8,128)(2,1)S(1)}, bf16[2,32,256]{2,1,0:T(8,128)(2,1)S(1)}) custom-call(s32[1]{0:T(128)} %bitcast.1.place_ref, bf16[32,512]{1,0:T(8,128)(2,1)S(1)} %residual.1.own_ref, bf16[32,512]{1,0:T(8,128)(2,1)S(1)} %collective-permute-done.10.other_ref, ...), custom_call_target="tpu_custom_call" | custom-call | tf_op jit(solution)/shard_map/mlp/pallas_call | solution.py:352
  93.5 0.4 collective-permute-start.11
  93.9 0.9 collective-permute-done.11.other_ref
  94.8 3.0 %collective-permute-start.12 = (f32[32,256]{1,0:T(8,128)S(1)}, f32[32,256]{1,0:T(8,128)S(1)}, u32[]{:S(2)}, u32[]{:S(2)}) collective-permute-start(f32[32,256]{1,0:T(8,128)S(1)} %get-tuple-element.38), channel_id=1, source_target_pairs={{0,2},{1,3},{2,0},{3,1},{4,6},{5,7},{6,4},{7,5},{8,10},{9,11},{10,... | collective-permute-start | bytes 98312 | tf_op jit(solution)/shard_map/ppermute | solution.py:383
  97.8 1.3 %collective-permute-done.12.other_ref = f32[32,256]{1,0:T(8,128)S(1)} collective-permute-done((f32[32,256]{1,0:T(8,128)S(1)}, f32[32,256]{1,0:T(8,128)S(1)}, u32[]{:S(2)}, u32[]{:S(2)}) %collective-permute-start.12) | collective-permute-done | bytes 32800 | tf_op jit(solution)/shard_map/ppermute | solution.py:383
  99.2 0.6 close.1
  (16 shorter events, 0.7 us)
Async XLA Ops:
  17.9 3.8 %collective-permute-start = (bf16[256,256]{1,0:T(8,128)(2,1)S(1)}, bf16[256,256]{1,0:T(8,128)(2,1)S(1)}, u32[]{:S(2)}, u32[]{:S(2)}) collective-permute-start(bf16[256,256]{1,0:T(8,128)(2,1)S(1)} %bitcast.2), channel_id=1, source_target_pairs={{0,4},{4,0},{1,5},{5,1},{2,6},{6,2},{3,7},{7,3},{8,12},{12,8},{9,1... | collective-permute-start | bytes 393224 | tf_op jit(solution)/shard_map/ppermute | solution.py:383
  21.7 11.0 %collective-permute-start.1 = (bf16[512,256]{1,0:T(8,128)(2,1)S(1)}, bf16[512,256]{1,0:T(8,128)(2,1)S(1)}, u32[]{:S(2)}, u32[]{:S(2)}) collective-permute-start(bf16[512,256]{1,0:T(8,128)(2,1)S(1)} %pad_maximum_fusion.refs_0_), channel_id=1, source_target_pairs={{0,128},{64,192},{128,0},{192,64},{1,129},{65,193},{129,1},{193,65... | collective-permute-start | bytes 786440 | tf_op jit(solution)/shard_map/ppermute | solution.py:378
  24.6 13.8 %collective-permute-start.3 = (bf16[512,256]{1,0:T(8,128)(2,1)S(1)}, bf16[512,256]{1,0:T(8,128)(2,1)S(1)}, u32[]{:S(2)}, u32[]{:S(2)}) collective-permute-start(bf16[512,256]{1,0:T(8,128)(2,1)S(1)} %pad_maximum_fusion.refs_0_), channel_id=1, source_target_pairs={{0,64},{64,128},{128,192},{192,0},{1,65},{65,129},{129,193},{193,1... | collective-permute-start | bytes 786440 | tf_op jit(solution)/shard_map/ppermute | solution.py:378
  24.9 20.4 %collective-permute-start.5 = (bf16[512,256]{1,0:T(8,128)(2,1)S(1)}, bf16[512,256]{1,0:T(8,128)(2,1)S(1)}, u32[]{:S(2)}, u32[]{:S(2)}) collective-permute-start(bf16[512,256]{1,0:T(8,128)(2,1)S(1)} %pad_maximum_fusion.refs_0_), channel_id=1, source_target_pairs={{0,192},{64,0},{128,64},{192,128},{1,193},{65,1},{129,65},{193,129... | collective-permute-start | bytes 786440 | tf_op jit(solution)/shard_map/ppermute | solution.py:378
  38.1 18.2 %collective-permute-start.2 = (bf16[544,256]{1,0:T(8,128)(2,1)S(1)}, bf16[544,256]{1,0:T(8,128)(2,1)S(1)}, u32[]{:S(2)}, u32[]{:S(2)}) collective-permute-start(bf16[544,256]{1,0:T(8,128)(2,1)S(1)} %attend.4), channel_id=1, source_target_pairs={{0,128},{64,192},{128,0},{192,64},{1,129},{65,193},{129,1},{193,65... | collective-permute-start | bytes 835592 | tf_op jit(solution)/shard_map/ppermute | solution.py:378
  43.7 12.6 %collective-permute-start.4 = (bf16[544,256]{1,0:T(8,128)(2,1)S(1)}, bf16[544,256]{1,0:T(8,128)(2,1)S(1)}, u32[]{:S(2)}, u32[]{:S(2)}) collective-permute-start(bf16[544,256]{1,0:T(8,128)(2,1)S(1)} %attend.5), channel_id=1, source_target_pairs={{0,192},{64,0},{128,64},{192,128},{1,193},{65,1},{129,65},{193,129... | collective-permute-start | bytes 835592 | tf_op jit(solution)/shard_map/ppermute | solution.py:378
  50.6 6.9 %collective-permute-start.6 = (bf16[544,256]{1,0:T(8,128)(2,1)S(1)}, bf16[544,256]{1,0:T(8,128)(2,1)S(1)}, u32[]{:S(2)}, u32[]{:S(2)}) collective-permute-start(bf16[544,256]{1,0:T(8,128)(2,1)S(1)} %attend.6), channel_id=1, source_target_pairs={{0,64},{64,128},{128,192},{192,0},{1,65},{65,129},{129,193},{193,1... | collective-permute-start | bytes 835592 | tf_op jit(solution)/shard_map/ppermute | solution.py:378
  56.3 18.1 %copy-start = (bf16[256,1024]{1,0:T(8,128)(2,1)S(1)}, bf16[256,1024]{1,0:T(8,128)(2,1)}, u32[]{:S(2)}) copy-start(bf16[256,1024]{1,0:T(8,128)(2,1)} %w_ref.1) | copy-start | bytes 1572868
  56.3 32.2 %copy-start.1 = (bf16[32,1024]{1,0:T(8,128)(2,1)S(1)}, bf16[32,1024]{1,0:T(8,128)(2,1)}, u32[]{:S(2)}) copy-start(bf16[32,1024]{1,0:T(8,128)(2,1)} %latent_ref.1) | copy-start | bytes 196612
  58.7 4.3 %collective-permute-start.7 = (bf16[272,256]{1,0:T(8,128)(2,1)S(1)}, bf16[272,256]{1,0:T(8,128)(2,1)S(1)}, u32[]{:S(2)}, u32[]{:S(2)}) collective-permute-start(bf16[272,256]{1,0:T(8,128)(2,1)S(1)} %get-tuple-element.28), channel_id=1, source_target_pairs={{0,4},{4,0},{1,5},{5,1},{2,6},{6,2},{3,7},{7,3},{8,12},{12,8},{9,1... | collective-permute-start | bytes 417800 | tf_op jit(solution)/shard_map/ppermute | solution.py:383
  74.8 9.0 %collective-permute-start.8 = (f32[32,512]{1,0:T(8,128)S(1)}, f32[32,512]{1,0:T(8,128)S(1)}, u32[]{:S(2)}, u32[]{:S(2)}) collective-permute-start(f32[32,512]{1,0:T(8,128)S(1)} %get-tuple-element.32), channel_id=1, source_target_pairs={{0,1},{1,0},{2,3},{3,2},{4,5},{5,4},{6,7},{7,6},{8,9},{9,8},{10,11... | collective-permute-start | bytes 196616 | tf_op jit(solution)/shard_map/ppermute | solution.py:383
  83.8 4.7 %collective-permute-start.9 = (f32[32,512]{1,0:T(8,128)S(1)}, f32[32,512]{1,0:T(8,128)S(1)}, u32[]{:S(2)}, u32[]{:S(2)}) collective-permute-start(f32[32,512]{1,0:T(8,128)S(1)} %pair_sum.1.one_ref), channel_id=1, source_target_pairs={{0,2},{1,3},{2,0},{3,1},{4,6},{5,7},{6,4},{7,5},{8,10},{9,11},{10,... | collective-permute-start | bytes 196616 | tf_op jit(solution)/shard_map/ppermute | solution.py:383
  88.5 2.4 %collective-permute-start.10 = (bf16[32,512]{1,0:T(8,128)(2,1)S(1)}, bf16[32,512]{1,0:T(8,128)(2,1)S(1)}, u32[]{:S(2)}, u32[]{:S(2)}) collective-permute-start(bf16[32,512]{1,0:T(8,128)(2,1)S(1)} %residual.1.own_ref), channel_id=1, source_target_pairs={{0,1},{1,0},{2,3},{3,2},{4,5},{5,4},{6,7},{7,6},{8,9},{9,8},{10,11... | collective-permute-start | bytes 98312 | tf_op jit(solution)/shard_map/ppermute | solution.py:383
  93.5 1.3 %collective-permute-start.11 = (bf16[2,32,256]{2,1,0:T(8,128)(2,1)S(1)}, bf16[2,32,256]{2,1,0:T(8,128)(2,1)S(1)}, u32[]{:S(2)}, u32[]{:S(2)}) collective-permute-start(bf16[2,32,256]{2,1,0:T(8,128)(2,1)S(1)} %get-tuple-element.36), channel_id=1, source_target_pairs={{0,1},{1,0},{2,3},{3,2},{4,5},{5,4},{6,7},{7,6},{8,9},{9,8},{10,11... | collective-permute-start | bytes 98312 | tf_op jit(solution)/shard_map/ppermute | solution.py:383
  94.8 4.4 %collective-permute-start.12 = (f32[32,256]{1,0:T(8,128)S(1)}, f32[32,256]{1,0:T(8,128)S(1)}, u32[]{:S(2)}, u32[]{:S(2)}) collective-permute-start(f32[32,256]{1,0:T(8,128)S(1)} %get-tuple-element.38), channel_id=1, source_target_pairs={{0,2},{1,3},{2,0},{3,1},{4,6},{5,7},{6,4},{7,5},{8,10},{9,11},{10,... | collective-permute-start | bytes 98312 | tf_op jit(solution)/shard_map/ppermute | solution.py:383

commit v3 on v2

--- a/solution.py
+++ b/solution.py
@@ -107,7 +107,7 @@
 
 def make_keys_values(x, w_key, w_value):
     tokens = x.shape[0]
-    block = 512
+    block = 1024
     return pl.pallas_call(
         functools.partial(key_value_kernel, block),
         in_specs=[pl.BlockSpec(memory_space=pltpu.HBM)] * 3,
@@ -121,7 +121,7 @@
             pltpu.VMEM(w_value.shape, BF16),
             pltpu.SemaphoreType.DMA((2 + tokens // block,)),
         ],
-        compiler_params=params(16),
+        compiler_params=params(24),
         name="make_keys_values",
     )(in_hbm(x), in_hbm(w_key), in_hbm(w_value))
 

time: 100 us -> 99.9 us (level)
  no operation moved by 1% of the time
where the time goes in v3:
time: 99.9 us; the launch traced here: 99.7 us
  Pallas kernels  33.1 us (33%)
  blocking collectives  27.6 us (28%)
  starting transfers between devices  26.4 us (26%)
  waiting for transfers between devices  12.3 us (12%)
    pallas_call x4, Pallas kernels, attend(): pl.pallas_call(functools.partial(attend_kernel, count, len(fetched)), in_...  21.3 us
    ppermute x7, starting transfers between devices, swapped(): return lax.ppermute(value, axes, [(i, i ^ bits) for i in range(size)])  18.8 us
    all_to_all x1, blocking collectives, on_device(): lax.all_to_all(spread, 'z', 0, 0, tiled=True).reshape(count * rows, columns)  16.6 us
    ppermute x7, waiting for transfers between devices, swapped(): return lax.ppermute(value, axes, [(i, i ^ bits) for i in range(size)])  11.1 us
    all_to_all x1, blocking collectives, on_device(): pieces = lax.all_to_all(block, 'z', 0, 0, tiled=True)  11 us
    ppermute x6, starting transfers between devices, along(): lax.ppermute(value, axis, [(i, (i + by) % size) for i in range(size)])  7.57 us
    pallas_call x1, Pallas kernels, make_keys_values(): pl.pallas_call(functools.partial(key_value_kernel, block), in_specs=[pl.B...  5.46 us
    pallas_call x1, Pallas kernels, mlp(): pl.pallas_call(mlp_kernel, in_specs=[pl.BlockSpec(memory_space=pltpu.SMEM...  2.5 us
  transfers between devices with their start and end apart: 13, of which 8 were waited for; matrix products, arithmetic and copies ran while one was open for 0% of the time, Pallas kernels for 27%

profile of v3, /device:TPU:1, one launch (start us, length us, event | category | flops | bytes accessed | tf_op | source)
XLA Modules:
  0.0 99.7 jit_solution(13070596795305000813)
XLA Ops:
  0.0 1.3 %make_queries.1 = bf16[32,256]{1,0:T(8,128)(2,1)S(1)} custom-call(bf16[32,1024]{1,0:T(8,128)(2,1)} %latent_ref.1, bf16[1024,256]{1,0:T(8,128)(2,1)} %w_hbm.1), custom_call_target="tpu_custom_call" | custom-call | tf_op jit(solution)/shard_map/make_queries/pallas_call | solution.py:58
  1.3 16.6 %all_to_all.10 = bf16[8,32,256]{2,1,0:T(8,128)(2,1)S(1)} all-to-all(bf16[8,32,256]{2,1,0:T(8,128)(2,1)S(1)} %broadcast_in_dim.2), channel_id=1, replica_groups=mesh['x'=4,'z'=8,'ylo'=2,'yhi'=2,'core'=2] {'z'}, dimensions={0} | all-to-all | bytes 262144 | tf_op jit(solution)/shard_map/all_to_all | solution.py:394
  17.9 1.3 %collective-permute-start = (bf16[256,256]{1,0:T(8,128)(2,1)S(1)}, bf16[256,256]{1,0:T(8,128)(2,1)S(1)}, u32[]{:S(2)}, u32[]{:S(2)}) collective-permute-start(bf16[256,256]{1,0:T(8,128)(2,1)S(1)} %bitcast.2), channel_id=1, source_target_pairs={{0,4},{4,0},{1,5},{5,1},{2,6},{6,2},{3,7},{7,3},{8,12},{12,8},{9,1... | collective-permute-start | bytes 393224 | tf_op jit(solution)/shard_map/ppermute | solution.py:383
  19.2 2.5 %collective-permute-done = bf16[256,256]{1,0:T(8,128)(2,1)S(1)} collective-permute-done((bf16[256,256]{1,0:T(8,128)(2,1)S(1)}, bf16[256,256]{1,0:T(8,128)(2,1)S(1)}, u32[]{:S(2)}, u32[]{:S(2)}) %collective-permute-start) | collective-permute-done | bytes 131104 | tf_op jit(solution)/shard_map/ppermute | solution.py:383
  21.7 2.8 %collective-permute-start.1 = (bf16[512,256]{1,0:T(8,128)(2,1)S(1)}, bf16[512,256]{1,0:T(8,128)(2,1)S(1)}, u32[]{:S(2)}, u32[]{:S(2)}) collective-permute-start(bf16[512,256]{1,0:T(8,128)(2,1)S(1)} %pad_maximum_fusion.refs_0_), channel_id=1, source_target_pairs={{0,128},{64,192},{128,0},{192,64},{1,129},{65,193},{129,1},{193,65... | collective-permute-start | bytes 786440 | tf_op jit(solution)/shard_map/ppermute | solution.py:378
  24.6 0.3 collective-permute-start.3
  24.9 2.4 %collective-permute-start.5 = (bf16[512,256]{1,0:T(8,128)(2,1)S(1)}, bf16[512,256]{1,0:T(8,128)(2,1)S(1)}, u32[]{:S(2)}, u32[]{:S(2)}) collective-permute-start(bf16[512,256]{1,0:T(8,128)(2,1)S(1)} %pad_maximum_fusion.refs_0_), channel_id=1, source_target_pairs={{0,192},{64,0},{128,64},{192,128},{1,193},{65,1},{129,65},{193,129... | collective-permute-start | bytes 786440 | tf_op jit(solution)/shard_map/ppermute | solution.py:378
  27.3 5.5 %make_keys_values.1 = (bf16[4,2048,64]{2,1,0:T(8,128)(2,1)S(1)}, bf16[4,2048,128]{2,1,0:T(8,128)(2,1)S(1)}) custom-call(bf16[2048,1024]{1,0:T(8,128)(2,1)} %x_hbm, bf16[1024,256]{1,0:T(8,128)(2,1)} %w_key_hbm.1, bf16[1024,256]{1,0:T(8,128)(2,1)} %w_value_hbm.1), custom_call_target="tpu_custom_call" | custom-call | tf_op jit(solution)/shard_map/make_keys_values/pallas_call | solution.py:111
  32.7 5.3 %attend.4 = bf16[544,256]{1,0:T(8,128)(2,1)S(1)} custom-call(bf16[512,256]{1,0:T(8,128)(2,1)S(1)} %collective-permute-done.1.refs_0_, bf16[4,2048,64]{2,1,0:T(8,128)(2,1)S(1)} %get-tuple-element.23.refs_1_, bf16[4,2048,128]{2,1,0:T(8,128)(2,1)S(1)} %get-tuple-element.24.refs_2_), custom_call_target="tpu_custom_call" | custom-call | tf_op jit(solution)/shard_map/attend/pallas_call | solution.py:199
  38.3 5.3 %attend.5 = bf16[544,256]{1,0:T(8,128)(2,1)S(1)} custom-call(bf16[512,256]{1,0:T(8,128)(2,1)S(1)} %collective-permute-done.3.refs_0_, bf16[4,2048,64]{2,1,0:T(8,128)(2,1)S(1)} %get-tuple-element.23.refs_1_, bf16[4,2048,128]{2,1,0:T(8,128)(2,1)S(1)} %get-tuple-element.24.refs_2_), custom_call_target="tpu_custom_call" | custom-call | tf_op jit(solution)/shard_map/attend/pallas_call | solution.py:199
  43.6 1.5 %collective-permute-start.4 = (bf16[544,256]{1,0:T(8,128)(2,1)S(1)}, bf16[544,256]{1,0:T(8,128)(2,1)S(1)}, u32[]{:S(2)}, u32[]{:S(2)}) collective-permute-start(bf16[544,256]{1,0:T(8,128)(2,1)S(1)} %attend.5), channel_id=1, source_target_pairs={{0,192},{64,0},{128,64},{192,128},{1,193},{65,1},{129,65},{193,129... | collective-permute-start | bytes 835592 | tf_op jit(solution)/shard_map/ppermute | solution.py:378
  45.2 5.3 %attend.6 = bf16[544,256]{1,0:T(8,128)(2,1)S(1)} custom-call(bf16[512,256]{1,0:T(8,128)(2,1)S(1)} %collective-permute-done.5.refs_0_, bf16[4,2048,64]{2,1,0:T(8,128)(2,1)S(1)} %get-tuple-element.23.refs_1_, bf16[4,2048,128]{2,1,0:T(8,128)(2,1)S(1)} %get-tuple-element.24.refs_2_), custom_call_target="tpu_custom_call" | custom-call | tf_op jit(solution)/shard_map/attend/pallas_call | solution.py:199
  50.8 5.3 %attend.7 = (bf16[544,256]{1,0:T(8,128)(2,1)S(1)}, bf16[1024,1024]{1,0:T(8,128)(2,1)S(1)}) custom-call(bf16[512,256]{1,0:T(8,128)(2,1)S(1)} %pad_maximum_fusion.refs_0_, bf16[4,2048,64]{2,1,0:T(8,128)(2,1)S(1)} %get-tuple-element.23.refs_1_, bf16[4,2048,128]{2,1,0:T(8,128)(2,1)S(1)} %get-tuple-element.24.refs_2_, bf16[1024,1024]{1,0:T(8,128)(2,1)} %refs_3_.1), custom_call_target="tpu_custom_call" | custom-call | tf_op jit(solution)/shard_map/attend/pallas_call | solution.py:199
  56.2 1.2 %collective-permute-done.6.refs_2_ = bf16[544,256]{1,0:T(8,128)(2,1)S(1)} collective-permute-done((bf16[544,256]{1,0:T(8,128)(2,1)S(1)}, bf16[544,256]{1,0:T(8,128)(2,1)S(1)}, u32[]{:S(2)}, u32[]{:S(2)}) %collective-permute-start.6) | collective-permute-done | bytes 278560 | tf_op jit(solution)/shard_map/ppermute | solution.py:378
  57.4 1.1 %merge.2 = (bf16[272,256]{1,0:T(8,128)(2,1)S(1)}, bf16[272,256]{1,0:T(8,128)(2,1)S(1)}) custom-call(bf16[544,256]{1,0:T(8,128)(2,1)S(1)} %collective-permute-done.2.refs_0_, bf16[544,256]{1,0:T(8,128)(2,1)S(1)} %collective-permute-done.4.refs_1_, bf16[544,256]{1,0:T(8,128)(2,1)S(1)} %collective-permute-done.6.refs_2_, ...), custom_call_target="tpu_custom_call" | custom-call | tf_op jit(solution)/shard_map/merge/pallas_call | solution.py:276
  58.5 1.3 %collective-permute-start.7 = (bf16[272,256]{1,0:T(8,128)(2,1)S(1)}, bf16[272,256]{1,0:T(8,128)(2,1)S(1)}, u32[]{:S(2)}, u32[]{:S(2)}) collective-permute-start(bf16[272,256]{1,0:T(8,128)(2,1)S(1)} %get-tuple-element.28), channel_id=1, source_target_pairs={{0,4},{4,0},{1,5},{5,1},{2,6},{6,2},{3,7},{7,3},{8,12},{12,8},{9,1... | collective-permute-start | bytes 417800 | tf_op jit(solution)/shard_map/ppermute | solution.py:383
  59.9 2.9 %collective-permute-done.7.refs_1_ = bf16[272,256]{1,0:T(8,128)(2,1)S(1)} collective-permute-done((bf16[272,256]{1,0:T(8,128)(2,1)S(1)}, bf16[272,256]{1,0:T(8,128)(2,1)S(1)}, u32[]{:S(2)}, u32[]{:S(2)}) %collective-permute-start.7) | collective-permute-done | bytes 139296 | tf_op jit(solution)/shard_map/ppermute | solution.py:383
  62.8 0.4 merge.3
  63.2 11.0 %all_to_all.11.pieces_ref = bf16[8,32,384]{2,1,0:T(8,128)(2,1)S(1)} all-to-all(bf16[8,32,384]{2,1,0:T(8,128)(2,1)S(1)} %merge.3), channel_id=1, replica_groups=mesh['x'=4,'z'=8,'ylo'=2,'yhi'=2,'core'=2] {'z'}, dimensions={0} | all-to-all | bytes 393216 | tf_op jit(solution)/shard_map/all_to_all | solution.py:409
  74.3 0.3 project.1
  74.6 8.2 %collective-permute-start.8 = (f32[32,512]{1,0:T(8,128)S(1)}, f32[32,512]{1,0:T(8,128)S(1)}, u32[]{:S(2)}, u32[]{:S(2)}) collective-permute-start(f32[32,512]{1,0:T(8,128)S(1)} %get-tuple-element.32), channel_id=1, source_target_pairs={{0,1},{1,0},{2,3},{3,2},{4,5},{5,4},{6,7},{7,6},{8,9},{9,8},{10,11... | collective-permute-start | bytes 196616 | tf_op jit(solution)/shard_map/ppermute | solution.py:383
  82.8 0.9 collective-permute-done.8.other_ref
  83.7 3.0 %collective-permute-start.9 = (f32[32,512]{1,0:T(8,128)S(1)}, f32[32,512]{1,0:T(8,128)S(1)}, u32[]{:S(2)}, u32[]{:S(2)}) collective-permute-start(f32[32,512]{1,0:T(8,128)S(1)} %pair_sum.1.one_ref), channel_id=1, source_target_pairs={{0,2},{1,3},{2,0},{3,1},{4,6},{5,7},{6,4},{7,5},{8,10},{9,11},{10,... | collective-permute-start | bytes 196616 | tf_op jit(solution)/shard_map/ppermute | solution.py:383
  86.7 1.7 %collective-permute-done.9.two_ref = f32[32,512]{1,0:T(8,128)S(1)} collective-permute-done((f32[32,512]{1,0:T(8,128)S(1)}, f32[32,512]{1,0:T(8,128)S(1)}, u32[]{:S(2)}, u32[]{:S(2)}) %collective-permute-start.9) | collective-permute-done | bytes 65568 | tf_op jit(solution)/shard_map/ppermute | solution.py:383
  88.5 1.6 %collective-permute-start.10 = (bf16[32,512]{1,0:T(8,128)(2,1)S(1)}, bf16[32,512]{1,0:T(8,128)(2,1)S(1)}, u32[]{:S(2)}, u32[]{:S(2)}) collective-permute-start(bf16[32,512]{1,0:T(8,128)(2,1)S(1)} %residual.1.own_ref), channel_id=1, source_target_pairs={{0,1},{1,0},{2,3},{3,2},{4,5},{5,4},{6,7},{7,6},{8,9},{9,8},{10,11... | collective-permute-start | bytes 98312 | tf_op jit(solution)/shard_map/ppermute | solution.py:383
  90.0 0.9 collective-permute-done.10.other_ref
  90.9 2.5 %mlp.1 = (bf16[4,32,256]{2,1,0:T(8,128)(2,1)S(1)}, bf16[2,32,256]{2,1,0:T(8,128)(2,1)S(1)}, bf16[2,32,256]{2,1,0:T(8,128)(2,1)S(1)}) custom-call(s32[1]{0:T(128)} %bitcast.1.place_ref, bf16[32,512]{1,0:T(8,128)(2,1)S(1)} %residual.1.own_ref, bf16[32,512]{1,0:T(8,128)(2,1)S(1)} %collective-permute-done.10.other_ref, ...), custom_call_target="tpu_custom_call" | custom-call | tf_op jit(solution)/shard_map/mlp/pallas_call | solution.py:352
  93.4 0.4 collective-permute-start.11
  93.9 0.9 collective-permute-done.11.other_ref
  94.7 3.0 %collective-permute-start.12 = (f32[32,256]{1,0:T(8,128)S(1)}, f32[32,256]{1,0:T(8,128)S(1)}, u32[]{:S(2)}, u32[]{:S(2)}) collective-permute-start(f32[32,256]{1,0:T(8,128)S(1)} %get-tuple-element.38), channel_id=1, source_target_pairs={{0,2},{1,3},{2,0},{3,1},{4,6},{5,7},{6,4},{7,5},{8,10},{9,11},{10,... | collective-permute-start | bytes 98312 | tf_op jit(solution)/shard_map/ppermute | solution.py:383
  97.7 1.4 %collective-permute-done.12.other_ref = f32[32,256]{1,0:T(8,128)S(1)} collective-permute-done((f32[32,256]{1,0:T(8,128)S(1)}, f32[32,256]{1,0:T(8,128)S(1)}, u32[]{:S(2)}, u32[]{:S(2)}) %collective-permute-start.12) | collective-permute-done | bytes 32800 | tf_op jit(solution)/shard_map/ppermute | solution.py:383
  99.1 0.6 close.1
  (16 shorter events, 0.6 us)
Async XLA Ops:
  17.9 3.8 %collective-permute-start = (bf16[256,256]{1,0:T(8,128)(2,1)S(1)}, bf16[256,256]{1,0:T(8,128)(2,1)S(1)}, u32[]{:S(2)}, u32[]{:S(2)}) collective-permute-start(bf16[256,256]{1,0:T(8,128)(2,1)S(1)} %bitcast.2), channel_id=1, source_target_pairs={{0,4},{4,0},{1,5},{5,1},{2,6},{6,2},{3,7},{7,3},{8,12},{12,8},{9,1... | collective-permute-start | bytes 393224 | tf_op jit(solution)/shard_map/ppermute | solution.py:383
  21.7 11.0 %collective-permute-start.1 = (bf16[512,256]{1,0:T(8,128)(2,1)S(1)}, bf16[512,256]{1,0:T(8,128)(2,1)S(1)}, u32[]{:S(2)}, u32[]{:S(2)}) collective-permute-start(bf16[512,256]{1,0:T(8,128)(2,1)S(1)} %pad_maximum_fusion.refs_0_), channel_id=1, source_target_pairs={{0,128},{64,192},{128,0},{192,64},{1,129},{65,193},{129,1},{193,65... | collective-permute-start | bytes 786440 | tf_op jit(solution)/shard_map/ppermute | solution.py:378
  24.6 13.7 %collective-permute-start.3 = (bf16[512,256]{1,0:T(8,128)(2,1)S(1)}, bf16[512,256]{1,0:T(8,128)(2,1)S(1)}, u32[]{:S(2)}, u32[]{:S(2)}) collective-permute-start(bf16[512,256]{1,0:T(8,128)(2,1)S(1)} %pad_maximum_fusion.refs_0_), channel_id=1, source_target_pairs={{0,64},{64,128},{128,192},{192,0},{1,65},{65,129},{129,193},{193,1... | collective-permute-start | bytes 786440 | tf_op jit(solution)/shard_map/ppermute | solution.py:378
  24.9 20.3 %collective-permute-start.5 = (bf16[512,256]{1,0:T(8,128)(2,1)S(1)}, bf16[512,256]{1,0:T(8,128)(2,1)S(1)}, u32[]{:S(2)}, u32[]{:S(2)}) collective-permute-start(bf16[512,256]{1,0:T(8,128)(2,1)S(1)} %pad_maximum_fusion.refs_0_), channel_id=1, source_target_pairs={{0,192},{64,0},{128,64},{192,128},{1,193},{65,1},{129,65},{193,129... | collective-permute-start | bytes 786440 | tf_op jit(solution)/shard_map/ppermute | solution.py:378
  38.1 18.1 %collective-permute-start.2 = (bf16[544,256]{1,0:T(8,128)(2,1)S(1)}, bf16[544,256]{1,0:T(8,128)(2,1)S(1)}, u32[]{:S(2)}, u32[]{:S(2)}) collective-permute-start(bf16[544,256]{1,0:T(8,128)(2,1)S(1)} %attend.4), channel_id=1, source_target_pairs={{0,128},{64,192},{128,0},{192,64},{1,129},{65,193},{129,1},{193,65... | collective-permute-start | bytes 835592 | tf_op jit(solution)/shard_map/ppermute | solution.py:378
  43.6 12.5 %collective-permute-start.4 = (bf16[544,256]{1,0:T(8,128)(2,1)S(1)}, bf16[544,256]{1,0:T(8,128)(2,1)S(1)}, u32[]{:S(2)}, u32[]{:S(2)}) collective-permute-start(bf16[544,256]{1,0:T(8,128)(2,1)S(1)} %attend.5), channel_id=1, source_target_pairs={{0,192},{64,0},{128,64},{192,128},{1,193},{65,1},{129,65},{193,129... | collective-permute-start | bytes 835592 | tf_op jit(solution)/shard_map/ppermute | solution.py:378
  50.5 6.9 %collective-permute-start.6 = (bf16[544,256]{1,0:T(8,128)(2,1)S(1)}, bf16[544,256]{1,0:T(8,128)(2,1)S(1)}, u32[]{:S(2)}, u32[]{:S(2)}) collective-permute-start(bf16[544,256]{1,0:T(8,128)(2,1)S(1)} %attend.6), channel_id=1, source_target_pairs={{0,64},{64,128},{128,192},{192,0},{1,65},{65,129},{129,193},{193,1... | collective-permute-start | bytes 835592 | tf_op jit(solution)/shard_map/ppermute | solution.py:378
  56.1 18.1 %copy-start = (bf16[256,1024]{1,0:T(8,128)(2,1)S(1)}, bf16[256,1024]{1,0:T(8,128)(2,1)}, u32[]{:S(2)}) copy-start(bf16[256,1024]{1,0:T(8,128)(2,1)} %w_ref.1) | copy-start | bytes 1572868
  56.2 32.3 %copy-start.1 = (bf16[32,1024]{1,0:T(8,128)(2,1)S(1)}, bf16[32,1024]{1,0:T(8,128)(2,1)}, u32[]{:S(2)}) copy-start(bf16[32,1024]{1,0:T(8,128)(2,1)} %latent_ref.1) | copy-start | bytes 196612
  58.5 4.3 %collective-permute-start.7 = (bf16[272,256]{1,0:T(8,128)(2,1)S(1)}, bf16[272,256]{1,0:T(8,128)(2,1)S(1)}, u32[]{:S(2)}, u32[]{:S(2)}) collective-permute-start(bf16[272,256]{1,0:T(8,128)(2,1)S(1)} %get-tuple-element.28), channel_id=1, source_target_pairs={{0,4},{4,0},{1,5},{5,1},{2,6},{6,2},{3,7},{7,3},{8,12},{12,8},{9,1... | collective-permute-start | bytes 417800 | tf_op jit(solution)/shard_map/ppermute | solution.py:383
  74.6 9.1 %collective-permute-start.8 = (f32[32,512]{1,0:T(8,128)S(1)}, f32[32,512]{1,0:T(8,128)S(1)}, u32[]{:S(2)}, u32[]{:S(2)}) collective-permute-start(f32[32,512]{1,0:T(8,128)S(1)} %get-tuple-element.32), channel_id=1, source_target_pairs={{0,1},{1,0},{2,3},{3,2},{4,5},{5,4},{6,7},{7,6},{8,9},{9,8},{10,11... | collective-permute-start | bytes 196616 | tf_op jit(solution)/shard_map/ppermute | solution.py:383
  83.7 4.7 %collective-permute-start.9 = (f32[32,512]{1,0:T(8,128)S(1)}, f32[32,512]{1,0:T(8,128)S(1)}, u32[]{:S(2)}, u32[]{:S(2)}) collective-permute-start(f32[32,512]{1,0:T(8,128)S(1)} %pair_sum.1.one_ref), channel_id=1, source_target_pairs={{0,2},{1,3},{2,0},{3,1},{4,6},{5,7},{6,4},{7,5},{8,10},{9,11},{10,... | collective-permute-start | bytes 196616 | tf_op jit(solution)/shard_map/ppermute | solution.py:383
  88.5 2.4 %collective-permute-start.10 = (bf16[32,512]{1,0:T(8,128)(2,1)S(1)}, bf16[32,512]{1,0:T(8,128)(2,1)S(1)}, u32[]{:S(2)}, u32[]{:S(2)}) collective-permute-start(bf16[32,512]{1,0:T(8,128)(2,1)S(1)} %residual.1.own_ref), channel_id=1, source_target_pairs={{0,1},{1,0},{2,3},{3,2},{4,5},{5,4},{6,7},{7,6},{8,9},{9,8},{10,11... | collective-permute-start | bytes 98312 | tf_op jit(solution)/shard_map/ppermute | solution.py:383
  93.4 1.3 %collective-permute-start.11 = (bf16[2,32,256]{2,1,0:T(8,128)(2,1)S(1)}, bf16[2,32,256]{2,1,0:T(8,128)(2,1)S(1)}, u32[]{:S(2)}, u32[]{:S(2)}) collective-permute-start(bf16[2,32,256]{2,1,0:T(8,128)(2,1)S(1)} %get-tuple-element.36), channel_id=1, source_target_pairs={{0,1},{1,0},{2,3},{3,2},{4,5},{5,4},{6,7},{7,6},{8,9},{9,8},{10,11... | collective-permute-start | bytes 98312 | tf_op jit(solution)/shard_map/ppermute | solution.py:383
  94.7 4.4 %collective-permute-start.12 = (f32[32,256]{1,0:T(8,128)S(1)}, f32[32,256]{1,0:T(8,128)S(1)}, u32[]{:S(2)}, u32[]{:S(2)}) collective-permute-start(f32[32,256]{1,0:T(8,128)S(1)} %get-tuple-element.38), channel_id=1, source_target_pairs={{0,2},{1,3},{2,0},{3,1},{4,6},{5,7},{6,4},{7,5},{8,10},{9,11},{10,... | collective-permute-start | bytes 98312 | tf_op jit(solution)/shard_map/ppermute | solution.py:383
